TPU v7x, 128 devices: a whole 4x4x4 slice. The times are simulated.
128 devices in a mesh: section: 2 (over core), tensor: 4 (over x), dp: 16 (over z, y).
Axes of the slice: x: 4, y: 4, z: 4, core: 2. Of those that a mesh axis runs over, the one named last changes fastest.
Arguments:
- boundary: float32 [2, 2, 2048, 1024], P('section', None, 'dp'), may hold values from -6 to 6
- doc_lengths: int32 [2, 16, 4], P(None, 'dp'), may hold values from 1 to 96, 128 in all within a row
- routes: int32 [2, 2, 2048, 8], P('section', None, 'dp'), may hold values from 0 to 31, all different within a row; in each aligned block of 128 rows (0 to 127, 128 to 255, ..., all dimensions but the last counted through in order) at most 48 rows name the same one
- norm_gains: bfloat16 [2, 2, 1024], P('section', None, 'dp'), may hold values from 0.5 to 1.5
- w_query: bfloat16 [2, 1024, 1024], P('section', 'dp', 'tensor'), may hold values from -0.1875 to 0.1875
- key_value_weight: bfloat16 [2, 2, 1024, 512], P('section', None, 'dp', 'tensor'), may hold values from -0.1875 to 0.1875
- w_out: bfloat16 [2, 1024, 1024], P('section', 'tensor', 'dp'), may hold values from -1 to 1
- w_router: bfloat16 [2, 1024, 32], P('section', 'dp'), may hold values from -0.09375 to 0.09375
- w_gateup: bfloat16 [2, 2, 32, 1024, 512], P('section', None, None, 'dp', 'tensor'), may hold values from -0.1875 to 0.1875
- w_down: bfloat16 [2, 32, 512, 1024], P('section', None, 'tensor', 'dp'), may hold values from -1.25 to 1.25
Outputs:
- layer_outputs: float32 [2, 2, 2048, 1024], P('section', None, 'dp')
- input_grads: float32 [2, 2, 2048, 1024], P('section', None, 'dp')
- grad_gains: float32 [2, 2, 1024], P('section', None, 'dp')
- grad_query: float32 [2, 1024, 1024], P('section', 'dp', 'tensor')
- grad_keyval: float32 [2, 2, 1024, 512], P('section', None, 'dp', 'tensor')
- grad_out: float32 [2, 1024, 1024], P('section', 'tensor', 'dp')
- grad_router: float32 [2, 1024, 32], P('section', 'dp')
- grad_gateup: float32 [2, 2, 32, 1024, 512], P('section', None, None, 'dp', 'tensor')
- grad_down: float32 [2, 32, 512, 1024], P('section', None, 'tensor', 'dp')
Inputs may be any that keep to these rules, and one draw needn't show every extreme that they name: `doc_lengths`: each group's 4 documents of a micro-batch fill its 128 rows; the longest has 96. `routes`: a token names 8 different experts; in each aligned block of 128 rows (one group's rows of one micro-batch and layer) no expert is named by more than 48 rows, a bound that some block reaches.
All inputs are finite; a program needn't handle non-finite values.
Results may differ from a plain program's by a relative error of at most 0.035.
Values may be sent and summed in bfloat16 or wider, within the bound.
A program may use at most 256 MiB of HBM per device.

v0:
```python
import jax
import jax.numpy as jnp
from jax import lax
from jax.sharding import PartitionSpec as P

HEAD_SIZE = 64
E = 32
TOPK = 8
CAP = 48


epsilon = 1e-06
rope_base = 10000.0
masked_score = -1e30


def from_everyone(x, axis):
    copies = jnp.broadcast_to(x, (lax.axis_size(axis), *x.shape))
    return lax.all_to_all(copies, axis, split_axis=0, concat_axis=0, tiled=True)


def over_copies(x, axis):
    everything = from_everyone(x, axis)
    return jnp.sum(everything.astype(jnp.float32), axis=0)


def shortened(x):

    def short(part):
        return part.astype(jnp.bfloat16) if part.dtype == jnp.float32 else part

    return jax.tree.map(short, x)


def rows_first(arrays, axis, dims):
    turned = [jnp.moveaxis(a, dim, 0) for a, dim in zip(arrays, dims)]
    widths = [t[0].size for t in turned]
    both = jnp.concatenate([t.reshape(-1, w) for t, w in zip(turned, widths)], axis=1)
    result = lax.all_gather(both, axis, axis=0, tiled=True)
    tiles = jnp.split(result, [sum(widths[:k]) for k in range(1, len(widths))], axis=1)
    return tuple(
        (
            jnp.moveaxis(b.reshape(-1, *t.shape[1:]), 0, dim)
            for b, t, dim in zip(tiles, turned, dims)
        )
    )


def from_behind(block, axis, distance):
    devices = range(lax.axis_size(axis))
    route = [(i - distance, i) for i in devices if i - distance in devices]
    return lax.ppermute(block, axis, route)


def split_up(x, dim, size):
    dims = x.shape
    tiles = x.reshape(*dims[:dim], size, dims[dim] // size, *dims[dim + 1 :])
    return jnp.moveaxis(tiles, dim, 0)


def sent_and_summed(x, axis, dim):
    tiles = split_up(x, dim, lax.axis_size(axis))
    arrived = lax.all_to_all(tiles, axis, split_axis=0, concat_axis=0, tiled=True)
    return arrived.astype(jnp.float32).sum(axis=0)


def doc_layout(lengths, count_of_rows):
    doc_ends = jnp.cumsum(lengths)
    doc_starts = doc_ends - lengths
    places = jnp.arange(count_of_rows, dtype=jnp.int32)
    segment = jnp.sum((places[:, None] >= doc_ends[None, :]).astype(jnp.int32), axis=1)
    owners = segment[:, None] == jnp.arange(lengths.shape[0], dtype=jnp.int32)[None, :]
    offset = places - jnp.sum(jnp.where(owners, doc_starts[None, :], 0), axis=1)
    visible = (segment[:, None] == segment[None, :]) & (places[None, :] <= places[:, None])
    return (offset, visible)


def rope_tables(offset, head_dim):
    half_dim = head_dim // 2
    frequency = rope_base ** (-2.0 * jnp.arange(half_dim, dtype=jnp.float32) / head_dim)
    angles = offset.astype(jnp.float32)[:, None] * frequency[None, :]
    return (jnp.cos(angles), jnp.sin(angles))


def rotate(values, cos_table, sin_table, head_dim):
    count_of_rows = values.shape[0]
    shaped = values.reshape(count_of_rows, -1, head_dim)
    first_half = shaped[..., : head_dim // 2]
    second_half = shaped[..., head_dim // 2 :]
    cos_view = cos_table[:, None, :]
    sin_view = sin_table[:, None, :]
    turned = jnp.concatenate(
        [
            first_half * cos_view - second_half * sin_view,
            second_half * cos_view + first_half * sin_view,
        ],
        axis=-1,
    )
    return turned.reshape(count_of_rows, -1)


def norm_apply(values, gain_row):
    scale_row = lax.rsqrt(jnp.mean(values * values, axis=1, keepdims=True) + epsilon)
    return (values * scale_row * gain_row[None, :], scale_row)


def norm_back(values, scale_row, gain_row, upstream):
    weighted = upstream * gain_row[None, :]
    inner = jnp.mean(weighted * values, axis=1, keepdims=True)
    back_rows = scale_row * weighted - values * scale_row * scale_row * scale_row * inner
    gain_grad = jnp.sum(upstream * values * scale_row, axis=0)
    return (back_rows, gain_grad)


def route_tables(routes, experts, capacity):
    pair_count = routes.shape[0] * routes.shape[1]
    flat_routes = routes.reshape(pair_count)
    onehot = (flat_routes[:, None] == jnp.arange(experts, dtype=jnp.int32)[None, :]).astype(
        jnp.int32
    )
    earlier = jnp.cumsum(onehot, axis=0) - onehot
    slot_index = jnp.sum(earlier * onehot, axis=1)
    pair_slot = flat_routes * capacity + slot_index
    slot_pair = (
        jnp.full((experts * capacity,), pair_count, jnp.int32)
        .at[pair_slot]
        .set(jnp.arange(pair_count, dtype=jnp.int32))
    )
    return (pair_slot, slot_pair)


def tensor_total(partial_rows):
    return over_copies(partial_rows.astype(jnp.bfloat16), "tensor").astype(jnp.float32)


def tensor_grads(partial_terms):
    return jax.tree.map(
        lambda part: part.astype(jnp.float32),
        jax.tree.map(lambda part: over_copies(part, "tensor"), shortened(partial_terms)),
    )


def attention_scores(query_reduced, key_reduced, visible):
    count_of_rows = query_reduced.shape[0]
    groups = key_reduced.shape[1] // HEAD_SIZE
    query_shaped_rows = query_reduced.reshape(count_of_rows, groups, -1, HEAD_SIZE)
    key_shaped_rows = key_reduced.reshape(count_of_rows, groups, HEAD_SIZE)
    scores = jnp.einsum(
        "qgrd,kgd->grqk", query_shaped_rows, key_shaped_rows, preferred_element_type=jnp.float32
    ) * HEAD_SIZE ** (-0.5)
    return jnp.where(visible[None, None], scores, masked_score)


def expert_apply(expert_in, w_gateup, w_down):
    gate_up = jnp.einsum("ecd,sedf->secf", expert_in, w_gateup, preferred_element_type=jnp.float32)
    hidden_low = (jax.nn.silu(gate_up[0]) * gate_up[1]).astype(jnp.bfloat16)
    expert_out = jnp.einsum("ecf,efd->ecd", hidden_low, w_down, preferred_element_type=jnp.float32)
    return (expert_out, (expert_in, gate_up, hidden_low))


def expert_grad_apply(out_grad, saved, w_gateup, w_down):
    expert_in, gate_up, hidden_low = saved
    hidden_grad = jnp.einsum("ecd,efd->ecf", out_grad, w_down, preferred_element_type=jnp.float32)
    sigmoid_gate = jax.nn.sigmoid(gate_up[0])
    gate_grad = hidden_grad * gate_up[1] * sigmoid_gate * (1.0 + gate_up[0] * (1.0 - sigmoid_gate))
    up_grad = hidden_grad * gate_up[0] * sigmoid_gate
    gate_up_grad = jnp.stack([gate_grad, up_grad]).astype(jnp.bfloat16)
    expert_back = jnp.einsum(
        "secf,sedf->ecd", gate_up_grad, w_gateup, preferred_element_type=jnp.float32
    )
    return (expert_back, (expert_in, gate_up_grad, hidden_low, out_grad))


def layer_forward(inputs, weights, routes, lengths, run_experts):
    gain_rows, w_query, key_value_weight, w_out, w_router = weights
    count_of_rows = inputs.shape[0]
    offset, visible = doc_layout(lengths, count_of_rows)
    cos_table, sin_table = rope_tables(offset, HEAD_SIZE)
    normed_one, scale_one = norm_apply(inputs, gain_rows[0].astype(jnp.float32))
    first_in = normed_one.astype(jnp.bfloat16)
    query_reduced = rotate(
        jnp.dot(first_in, w_query, preferred_element_type=jnp.float32),
        cos_table,
        sin_table,
        HEAD_SIZE,
    ).astype(jnp.bfloat16)
    key_value = jnp.einsum(
        "nd,sdh->snh", first_in, key_value_weight, preferred_element_type=jnp.float32
    )
    key_reduced = rotate(key_value[0], cos_table, sin_table, HEAD_SIZE).astype(jnp.bfloat16)
    value_reduced = key_value[1].astype(jnp.bfloat16)
    scores = attention_scores(query_reduced, key_reduced, visible)
    row_peak = jnp.max(scores, axis=-1, keepdims=True)
    raised = jnp.exp(scores - row_peak)
    totals = jnp.sum(raised, axis=-1, keepdims=True)
    log_total = row_peak + jnp.log(totals)
    prob_low = (raised / totals).astype(jnp.bfloat16)
    groups = value_reduced.shape[1] // HEAD_SIZE
    mixed_rows = jnp.einsum(
        "grqk,kgd->qgrd",
        prob_low,
        value_reduced.reshape(count_of_rows, groups, HEAD_SIZE),
        preferred_element_type=jnp.float32,
    )
    mixed_low = mixed_rows.reshape(count_of_rows, -1).astype(jnp.bfloat16)
    attended = tensor_total(jnp.dot(mixed_low, w_out, preferred_element_type=jnp.float32))
    middle = inputs + attended
    normed_two, scale_two = norm_apply(middle, gain_rows[1].astype(jnp.float32))
    second_in = normed_two.astype(jnp.bfloat16)
    logits = jnp.dot(second_in, w_router, preferred_element_type=jnp.float32)
    picker = (routes[:, :, None] == jnp.arange(E, dtype=jnp.int32)[None, None, :]).astype(
        jnp.float32
    )
    picked = jnp.sum(picker * logits[:, None, :], axis=-1)
    gate_probs = jax.nn.softmax(picked, axis=-1)
    pair_slot, slot_pair = route_tables(routes, E, CAP)
    padded = jnp.concatenate([second_in, jnp.zeros((1, second_in.shape[1]), jnp.bfloat16)], axis=0)
    expert_in = padded[slot_pair // TOPK].reshape(E, CAP, -1)
    expert_out, expert_saved = run_experts(expert_in)
    pair_out = expert_out.reshape(E * CAP, -1)[pair_slot].reshape(count_of_rows, TOPK, -1)
    mixture = tensor_total(jnp.sum(gate_probs[:, :, None] * pair_out, axis=1))
    produced = middle + mixture
    kept_state = (
        inputs,
        scale_one,
        first_in,
        query_reduced,
        key_reduced,
        value_reduced,
        log_total,
        visible,
        cos_table,
        sin_table,
        mixed_low,
        middle,
        scale_two,
        second_in,
        picker,
        gate_probs,
        pair_slot,
        slot_pair,
        expert_saved,
        pair_out,
    )
    return (produced, kept_state)


def layer_backward(kept_state, weights, upstream, back_experts):
    (
        inputs,
        scale_one,
        first_in,
        query_reduced,
        key_reduced,
        value_reduced,
        log_total,
        visible,
        cos_table,
        sin_table,
        mixed_low,
        middle,
        scale_two,
        second_in,
        picker,
        gate_probs,
        pair_slot,
        slot_pair,
        expert_saved,
        pair_out,
    ) = kept_state
    gain_rows, w_query, key_value_weight, w_out, w_router = weights
    count_of_rows = upstream.shape[0]
    pair_grad = (gate_probs[:, :, None] * upstream[:, None, :]).astype(jnp.bfloat16)
    gate_part = jnp.sum(pair_out * upstream[:, None, :], axis=-1)
    padded_grad = jnp.concatenate(
        [
            pair_grad.reshape(count_of_rows * TOPK, -1),
            jnp.zeros((1, upstream.shape[1]), jnp.bfloat16),
        ],
        axis=0,
    )
    out_grad = padded_grad[slot_pair].reshape(E, CAP, -1)
    expert_back, expert_deferred = back_experts(out_grad, expert_saved)
    token_back = jnp.sum(
        expert_back.reshape(E * CAP, -1)[pair_slot].reshape(count_of_rows, TOPK, -1), axis=1
    )
    summed_back, gate_total = tensor_grads((token_back, gate_part))
    picked_grad = gate_probs * (
        gate_total - jnp.sum(gate_probs * gate_total, axis=-1, keepdims=True)
    )
    logit_low = jnp.sum(picker * picked_grad[:, :, None], axis=1).astype(jnp.bfloat16)
    router_back = jnp.einsum("ne,de->nd", logit_low, w_router, preferred_element_type=jnp.float32)
    norm_two_back, gain_two_grad = norm_back(
        middle, scale_two, gain_rows[1].astype(jnp.float32), summed_back + router_back
    )
    resid_grad = upstream + norm_two_back
    branch_low = resid_grad.astype(jnp.bfloat16)
    mixed_grad = jnp.einsum(
        "nd,hd->nh", branch_low, w_out, preferred_element_type=jnp.float32
    ).astype(jnp.bfloat16)
    groups = key_reduced.shape[1] // HEAD_SIZE
    scores = attention_scores(query_reduced, key_reduced, visible)
    prob_rows = jnp.exp(scores - log_total)
    prob_low = prob_rows.astype(jnp.bfloat16)
    query_shaped_rows = query_reduced.reshape(count_of_rows, groups, -1, HEAD_SIZE)
    key_shaped_rows = key_reduced.reshape(count_of_rows, groups, HEAD_SIZE)
    value_shaped_rows = value_reduced.reshape(count_of_rows, groups, HEAD_SIZE)
    grad_view = mixed_grad.reshape(count_of_rows, groups, -1, HEAD_SIZE)
    value_grad = (
        jnp.einsum("grqk,qgrd->kgd", prob_low, grad_view, preferred_element_type=jnp.float32)
        .reshape(count_of_rows, -1)
        .astype(jnp.bfloat16)
    )
    prob_grad = jnp.einsum(
        "qgrd,kgd->grqk", grad_view, value_shaped_rows, preferred_element_type=jnp.float32
    )
    score_low = (
        prob_rows * (prob_grad - jnp.sum(prob_rows * prob_grad, axis=-1, keepdims=True))
    ).astype(jnp.bfloat16)
    score_scale = HEAD_SIZE ** (-0.5)
    query_grad = (
        jnp.einsum(
            "grqk,kgd->qgrd", score_low, key_shaped_rows, preferred_element_type=jnp.float32
        ).reshape(count_of_rows, -1)
        * score_scale
    )
    key_grad = (
        jnp.einsum(
            "grqk,qgrd->kgd", score_low, query_shaped_rows, preferred_element_type=jnp.float32
        ).reshape(count_of_rows, -1)
        * score_scale
    )
    query_pre_low = rotate(query_grad, cos_table, -sin_table, HEAD_SIZE).astype(jnp.bfloat16)
    key_pre_low = rotate(key_grad, cos_table, -sin_table, HEAD_SIZE).astype(jnp.bfloat16)
    keyval_low = jnp.stack([key_pre_low, value_grad])
    first_back = jnp.einsum(
        "nh,dh->nd", query_pre_low, w_query, preferred_element_type=jnp.float32
    ) + jnp.einsum("snh,sdh->nd", keyval_low, key_value_weight, preferred_element_type=jnp.float32)
    first_sum = tensor_grads((first_back,))[0]
    norm_one_back, gain_one_grad = norm_back(
        inputs, scale_one, gain_rows[0].astype(jnp.float32), first_sum
    )
    input_grad = resid_grad + norm_one_back
    deferred = (
        first_in,
        query_pre_low,
        keyval_low,
        mixed_low,
        branch_low,
        second_in,
        logit_low,
    ) + expert_deferred
    return (input_grad, jnp.stack([gain_one_grad, gain_two_grad]), deferred)


def local(
    boundary,
    doc_lengths,
    routes,
    norm_gains,
    w_query,
    key_value_weight,
    w_out,
    w_router,
    w_gateup,
    w_down,
):
    micro_count = boundary.shape[1]
    first_section = lax.axis_index("section") == 0
    weights = (
        lax.all_gather(norm_gains[0], "dp", axis=1, tiled=True),
        lax.all_gather(w_query[0], "dp", axis=0, tiled=True),
        lax.all_gather(key_value_weight[0], "dp", axis=1, tiled=True),
        lax.all_gather(w_out[0], "dp", axis=1, tiled=True),
        lax.all_gather(w_router[0], "dp", axis=0, tiled=True),
    )
    expert_weights = rows_first((w_gateup[0], w_down[0]), "dp", (2, 2))

    def run_experts(expert_in):
        return expert_apply(expert_in, expert_weights[0], expert_weights[1])

    def back_experts(out_grad, saved):
        return expert_grad_apply(out_grad, saved, expert_weights[0], expert_weights[1])

    received = jnp.zeros_like(boundary[0, 0])
    kept_list = []
    produced_list = []
    for tick_no in range(micro_count + 1):
        early = min(tick_no, micro_count - 1)
        late = max(tick_no - 1, 0)
        layer_in = jnp.where(first_section, boundary[0, early], received)
        lengths_now = jnp.where(first_section, doc_lengths[early, 0], doc_lengths[late, 0])
        routes_now = jnp.where(first_section, routes[0, early], routes[0, late])
        produced, kept_state = layer_forward(
            layer_in, weights, routes_now, lengths_now, run_experts
        )
        kept_list.append(kept_state)
        produced_list.append(produced)
        if tick_no < micro_count:
            received = from_behind(produced.astype(jnp.bfloat16), "section", 1).astype(
                produced.dtype
            )
    layer_outputs = jnp.stack(
        [
            jnp.where(first_section, produced_list[index_mb], produced_list[index_mb + 1])
            for index_mb in range(micro_count)
        ]
    )
    received = jnp.zeros_like(boundary[0, 0])
    grad_list = []
    deferred_list = []
    gain_total = jnp.zeros((2, boundary.shape[3]), jnp.float32)
    for tick_no in range(micro_count + 1):
        kept_state = kept_list[micro_count - tick_no]
        if tick_no < micro_count:
            own_grad = boundary[0, micro_count - 1 - tick_no]
        else:
            own_grad = jnp.zeros_like(received)
        upstream = jnp.where(first_section, received, own_grad)
        input_grad, gain_grad, deferred = layer_backward(
            kept_state, weights, upstream, back_experts
        )
        grad_list.append(input_grad)
        deferred_list.append(deferred)
        gain_total = gain_total + gain_grad
        if tick_no < micro_count:
            received = from_behind(input_grad.astype(jnp.bfloat16), "section", -1).astype(
                input_grad.dtype
            )
    input_grads = jnp.stack(
        [
            jnp.where(
                first_section,
                grad_list[micro_count - index_mb],
                grad_list[micro_count - 1 - index_mb],
            )
            for index_mb in range(micro_count)
        ]
    )
    row_axes = (0, 0, 1, 0, 0, 0, 0, 1, 2, 1, 1)
    joined = [
        jnp.concatenate([entry[position] for entry in deferred_list], axis=row_axes[position])
        for position in range(11)
    ]
    (
        first_all,
        query_all,
        keyval_all,
        mixed_all,
        branch_all,
        second_all,
        logit_all,
        expert_all,
        gate_up_all,
        hidden_all,
        out_all,
    ) = joined
    grad_query = jnp.einsum("nd,nh->dh", first_all, query_all, preferred_element_type=jnp.float32)
    grad_keyval = jnp.einsum(
        "nd,snh->sdh", first_all, keyval_all, preferred_element_type=jnp.float32
    )
    grad_out = jnp.einsum("nh,nd->hd", mixed_all, branch_all, preferred_element_type=jnp.float32)
    grad_router = jnp.einsum("nd,ne->de", second_all, logit_all, preferred_element_type=jnp.float32)
    grad_gateup = jnp.einsum(
        "ecd,secf->sedf", expert_all, gate_up_all, preferred_element_type=jnp.float32
    )
    grad_down = jnp.einsum("ecf,ecd->efd", hidden_all, out_all, preferred_element_type=jnp.float32)
    dense = (
        sent_and_summed(gain_total.astype(jnp.bfloat16), "dp", 1),
        sent_and_summed(grad_query.astype(jnp.bfloat16), "dp", 0),
        sent_and_summed(grad_keyval.astype(jnp.bfloat16), "dp", 1),
        sent_and_summed(grad_out.astype(jnp.bfloat16), "dp", 1),
        sent_and_summed(grad_router.astype(jnp.bfloat16), "dp", 0),
    )
    summed = (
        lax.psum_scatter(
            grad_gateup.astype(jnp.bfloat16), "dp", scatter_dimension=2, tiled=True
        ).astype(jnp.float32),
        lax.psum_scatter(
            grad_down.astype(jnp.bfloat16), "dp", scatter_dimension=2, tiled=True
        ).astype(jnp.float32),
    )
    gateup_part = summed[0]
    down_part = summed[1]
    return (
        layer_outputs[None],
        input_grads[None],
        dense[0][None],
        dense[1][None],
        dense[2][None],
        dense[3][None],
        dense[4][None],
        gateup_part[None],
        down_part[None],
    )


def solution(mesh):
    placed = (
        P("section", None, "dp", None),
        P(None, "dp", None),
        P("section", None, "dp", None),
        P("section", None, "dp"),
        P("section", "dp", "tensor"),
        P("section", None, "dp", "tensor"),
        P("section", "tensor", "dp"),
        P("section", "dp", None),
        P("section", None, None, "dp", "tensor"),
        P("section", None, "tensor", "dp"),
    )
    return jax.shard_map(
        local,
        mesh=mesh,
        in_specs=placed,
        out_specs=(
            P("section", None, "dp", None),
            P("section", None, "dp", None),
            P("section", None, "dp"),
            P("section", "dp", "tensor"),
            P("section", None, "dp", "tensor"),
            P("section", "tensor", "dp"),
            P("section", "dp", None),
            P("section", None, None, "dp", "tensor"),
            P("section", None, "tensor", "dp"),
        ),
        check_vma=False,
    )
```

profile of v0, /device:TPU:0, one launch (start us, length us, event | category | flops | bytes accessed | tf_op | source)
XLA Modules:
  0.0 921.8 jit_solution(15594674634499253965)
XLA Ops:
  12.4 26.5 %all-gather.1 = bf16[1,2,1024,128]{3,1,0,2:T(2,128)(2,1)S(1)} all-gather(bf16[1,2,64,128]{3,1,0,2:T(2,128)(2,1)S(1)} %copy.435), channel_id=3, replica_groups=mesh['section'=2,'tensor'=4,'dp'=16] {'dp'}, dimensions={2}, use_global_device_ids=true | all-gather | bytes 557056 | tf_op jit(solution)/shard_map/all_gather | solution.py:373
  39.4 24.3 %all-gather = bf16[1,2,1024]{1,0,2:T(2,128)(2,1)S(1)} all-gather(bf16[1,2,64]{1,0,2:T(2,128)(2,1)S(1)} %copy.434), channel_id=2, replica_groups=mesh['section'=2,'tensor'=4,'dp'=16] {'dp'}, dimensions={2}, use_global_device_ids=true | all-gather | bytes 4352 | tf_op jit(solution)/shard_map/all_gather | solution.py:371
  71.2 23.0 %all-gather.2 = bf16[1,1024,256]{2,1,0:T(8,128)(2,1)S(1)} all-gather(bf16[1,64,256]{2,1,0:T(8,128)(2,1)S(1)} %copy-done.150), channel_id=4, replica_groups=mesh['section'=2,'tensor'=4,'dp'=16] {'dp'}, dimensions={1}, use_global_device_ids=true | all-gather | bytes 557056 | tf_op jit(solution)/shard_map/all_gather | solution.py:372
  96.3 24.4 %all-gather.3 = bf16[1,256,1024]{1,2,0:T(8,128)(2,1)S(1)} all-gather(bf16[1,256,64]{1,2,0:T(8,128)(2,1)S(1)} %copy-done.151), channel_id=5, replica_groups=mesh['section'=2,'tensor'=4,'dp'=16] {'dp'}, dimensions={2}, use_global_device_ids=true | all-gather | bytes 557056 | tf_op jit(solution)/shard_map/all_gather | solution.py:374
  137.8 25.0 %all-gather.4 = bf16[1,1024,32]{2,0,1:T(2,128)(2,1)} all-gather(bf16[1,64,32]{2,0,1:T(2,128)(2,1)S(1)} %copy.439), channel_id=6, replica_groups=mesh['section'=2,'tensor'=4,'dp'=16] {'dp'}, dimensions={1}, use_global_device_ids=true | all-gather | bytes 69632 | tf_op jit(solution)/shard_map/all_gather | solution.py:375
  181.8 13.9 %split.8 = bf16[1024,8192]{1,0:T(8,128)(2,1)} slice(bf16[1024,12288]{1,0:T(8,128)(2,1)} %all-gather.7.cloned.1.call-done), slice={[0:1024], [0:8192]} | slice | bytes 33554432 | tf_op jit(solution)/shard_map/split | solution.py:40
  195.7 22.4 %copy.444 = bf16[1024,8192]{0,1:T(8,128)(2,1)} copy(bf16[1024,8192]{1,0:T(8,128)(2,1)} %split.8) | data formatting | bytes 33554432 | tf_op jit(solution)/shard_map/split | solution.py:40
  225.9 12.0 %copy.452 = bf16[1024,4096]{0,1:T(8,128)(2,1)} copy(bf16[1024,4096]{1,0:T(8,128)(2,1)} %split.9) | data formatting | bytes 16777216 | tf_op jit(solution)/shard_map/split | solution.py:40
  237.9 22.5 %copy.445 = bf16[1024,2,32,128]{3,0,1,2:T(8,128)(2,1)} copy(bf16[1024,2,32,128]{0,3,2,1:T(8,128)(2,1)} %bitcast.650) | data formatting | bytes 33554432 | tf_op jit(solution)/shard_map/reshape | solution.py:43
  260.4 9.5 %fusion.25 = f32[2,32,48,128]{3,2,0,1:T(8,128)S(1)} fusion(bf16[32,48,1024,1]{2,1,3,0:T(8,128)(2,1)} %bitcast.676, bf16[1024,2,32,128]{3,0,1,2:T(8,128)(2,1)} %copy.445), kind=kOutput, calls=%fused_computation.66 | convolution fusion | flops 805306368 | bytes 21495808 | tf_op jit(solution)/shard_map/ecd,sedf->secf/dot_general | solution.py:155
  326.6 10.9 %all-to-all-done.2 = bf16[4,128,1024]{2,1,0:T(8,128)(2,1)} async-done(((bf16[4,128,1024]{2,1,0:T(8,128)(2,1)}), bf16[4,128,1024]{2,1,0:T(8,128)(2,1)}, u32[]{:S(2)}, u32[]{:S(2)}) %all-to-all-start.2) | async-done | bytes 1048608 | tf_op jit(solution)/shard_map/all_to_all | solution.py:19
  346.4 13.1 %convolution_bitcast_fusion.1 = f32[2,32,48,128]{3,2,1,0:T(8,128)} fusion(bf16[32,48,1024,1]{2,1,0,3:T(8,128)(2,1)} %bitcast.678, bf16[2,32,1024,128]{2,3,1,0:T(8,128)(2,1)} %bitcast.651), kind=kOutput, calls=%fused_computation.68 | convolution fusion | flops 805306368 | bytes 21495808 | tf_op jit(solution)/shard_map/ecd,sedf->secf/dot_general | solution.py:155
  368.4 9.2 gather_fusion.3
  386.7 15.1 %all-to-all-done.3 = bf16[4,128,1024]{2,1,0:T(8,128)(2,1)} async-done(((bf16[4,128,1024]{2,1,0:T(8,128)(2,1)}), bf16[4,128,1024]{2,1,0:T(8,128)(2,1)}, u32[]{:S(2)}, u32[]{:S(2)}) %all-to-all-start.3) | async-done | bytes 1048608 | tf_op jit(solution)/shard_map/all_to_all | solution.py:19
  448.3 13.1 %convolution_bitcast_fusion = f32[2,32,48,128]{3,2,1,0:T(8,128)} fusion(bf16[32,48,1024,1]{2,1,0,3:T(8,128)(2,1)} %bitcast.680, bf16[2,32,1024,128]{2,3,1,0:T(8,128)(2,1)} %bitcast.652), kind=kOutput, calls=%fused_computation.67 | convolution fusion | flops 805306368 | bytes 21495808 | tf_op jit(solution)/shard_map/ecd,sedf->secf/dot_general | solution.py:155
  487.7 9.1 gather_fusion.7
  496.9 9.5 %gather_fusion.5 = f32[1024,1024]{1,0:T(8,128)} fusion(f32[1536,1024]{1,0:T(8,128)} %bitcast.666, s32[1024]{0:T(1024)S(1)} %copy-done.129), kind=kCustom, calls=%fused_computation.5 | custom fusion | bytes 8392704 | tf_op jit(solution)/shard_map/gather | solution.py:220
  525.4 10.3 %all-to-all-done.6 = bf16[4,128,1024]{2,1,0:T(8,128)(2,1)} async-done(((bf16[4,128,1024]{2,1,0:T(8,128)(2,1)}), bf16[4,128,1024]{2,1,0:T(8,128)(2,1)}, u32[]{:S(2)}, u32[]{:S(2)}) %all-to-all-start.6) | async-done | bytes 1048608 | tf_op jit(solution)/shard_map/all_to_all | solution.py:19
  563.1 13.4 %all_to_all.100 = bf16[4,128,1024]{2,1,0:T(8,128)(2,1)S(1)} all-to-all(bf16[4,128,1024]{2,1,0:T(8,128)(2,1)S(1)} %broadcast_in_dim.147), channel_id=1, replica_groups=mesh['section'=2,'tensor'=4,'dp'=16] {'tensor'}, dimensions={0} | all-to-all | bytes 2097152 | tf_op jit(solution)/shard_map/all_to_all | solution.py:19
  603.3 11.7 %fusion.56 = f32[32,48,1024,1]{2,1,0,3:T(8,128)} fusion(bf16[2,32,1024,128]{2,3,1,0:T(8,128)(2,1)} %bitcast.653, bf16[1,32,48,128]{3,2,1,0:T(8,128)(2,1)S(1)} %get-tuple-element.115, bf16[1,32,48,128]{3,2,1,0:T(8,128)(2,1)S(1)} %get-tuple-element.114), kind=kOutput, calls=%fused_computation.147 | convolution fusion | flops 805699584 | bytes 23855104 | tf_op jit(solution)/shard_map/secf,sedf->ecd/dot_general | solution.py:168
  615.1 9.2 %gather_fusion.9 = f32[1024,1024]{1,0:T(8,128)} fusion(f32[1536,1024]{1,0:T(8,128)} %bitcast.670, s32[1024]{0:T(1024)S(1)} %copy-done.128), kind=kCustom, calls=%fused_computation.9 | custom fusion | bytes 8392704 | tf_op jit(solution)/shard_map/gather | solution.py:285
  634.6 14.4 %all-to-all-done.9 = bf16[4,128,1024]{2,1,0:T(8,128)(2,1)} async-done(((bf16[4,128,1024]{2,1,0:T(8,128)(2,1)}), bf16[4,128,1024]{2,1,0:T(8,128)(2,1)}, u32[]{:S(2)}, u32[]{:S(2)}) %all-to-all-start.9) | async-done | bytes 1048608 | tf_op jit(solution)/shard_map/all_to_all | solution.py:19
  658.1 16.6 %all_to_all.101 = bf16[4,128,1024]{2,1,0:T(8,128)(2,1)S(1)} all-to-all(bf16[4,128,1024]{2,1,0:T(8,128)(2,1)S(1)} %broadcast_in_dim.151), channel_id=1, replica_groups=mesh['section'=2,'tensor'=4,'dp'=16] {'tensor'}, dimensions={0} | all-to-all | bytes 2097152 | tf_op jit(solution)/shard_map/all_to_all | solution.py:19
  687.1 9.7 %fusion.12 = bf16[32,128,1024]{1,2,0:T(8,128)(2,1)} fusion(bf16[32,48,1024]{2,1,0:T(8,128)(2,1)} %bitcast.688, bf16[32,48,1024]{2,1,0:T(8,128)(2,1)} %bitcast.687, bf16[32,48,1024]{2,1,0:T(8,128)(2,1)} %bitcast.685, bf16[32,48,128]{2,1,0:T(8,128)(2,1)} %copy-done.40, bf16[32,48,128]{2,1,0:T(8,128)(2,1)} %copy-done.41, bf16[32,48,128]{2,1,0:T(8,128)(2,1)} %copy-done.59), kind=kOutput, calls=%fused_computation.29 | convolution fusion | flops 1244004352 | bytes 19005440 | tf_op jit(solution)/shard_map/ecf,ecd->efd/dot_general | solution.py:467
  706.7 9.6 %convert_bitcast_fusion = bf16[2,32,1024,128]{2,3,0,1:T(8,128)(2,1)} fusion(bf16[32,48,1024]{2,1,0:T(8,128)(2,1)S(1)} %bitcast.677, bf16[32,48,1024]{2,1,0:T(8,128)(2,1)S(1)} %bitcast.679, bf16[32,48,1024]{2,1,0:T(8,128)(2,1)S(1)} %bitcast.681, bf16[1,32,48,128]{3,2,1,0:T(8,128)(2,1)} %get-tuple-element.113, ...), kind=kOutput, calls=%fused_computation.17 | convolution fusion | flops 2466775040 | bytes 28573696 | tf_op jit(solution)/shard_map/ecd,secf->sedf/dot_general | solution.py:464
  716.3 24.3 %copy.505 = bf16[2,32,1024,128]{3,1,0,2:T(8,128)(2,1)} copy(bf16[2,32,1024,128]{2,3,0,1:T(8,128)(2,1)} %convert_bitcast_fusion) | data formatting | bytes 33554432 | tf_op jit(solution)/shard_map/convert_element_type | solution.py:477
  748.8 11.7 %fusion.60 = f32[32,48,1024,1]{2,1,0,3:T(8,128)} fusion(bf16[2,32,1024,128]{2,3,1,0:T(8,128)(2,1)} %bitcast.654, bf16[1,32,48,128]{3,2,1,0:T(8,128)(2,1)S(1)} %copy-done.92, bf16[1,32,48,128]{3,2,1,0:T(8,128)(2,1)S(1)} %copy-done.91), kind=kOutput, calls=%fused_computation.151 | convolution fusion | flops 805699584 | bytes 23855104 | tf_op jit(solution)/shard_map/secf,sedf->ecd/dot_general | solution.py:168
  760.5 9.2 %gather_fusion.11 = f32[1024,1024]{1,0:T(8,128)} fusion(f32[1536,1024]{1,0:T(8,128)} %bitcast.669, s32[1024]{0:T(1024)S(1)} %copy-done.126), kind=kCustom, calls=%fused_computation.11 | custom fusion | bytes 8392704 | tf_op jit(solution)/shard_map/gather | solution.py:285
  782.2 12.1 %all-to-all-done.12 = bf16[4,128,1024]{2,1,0:T(8,128)(2,1)} async-done(((bf16[4,128,1024]{2,1,0:T(8,128)(2,1)}), bf16[4,128,1024]{2,1,0:T(8,128)(2,1)}, u32[]{:S(2)}, u32[]{:S(2)}) %all-to-all-start.12) | async-done | bytes 1048608 | tf_op jit(solution)/shard_map/all_to_all | solution.py:19
  817.8 14.2 %all-to-all-done.18 = bf16[16,256,64]{1,2,0:T(8,128)(2,1)S(1)} async-done(((bf16[16,256,64]{1,2,0:T(8,128)(2,1)}), bf16[16,256,64]{1,2,0:T(8,128)(2,1)S(1)}, u32[]{:S(2)}, u32[]{:S(2)}) %all-to-all-start.18) | async-done | bytes 524320 | tf_op jit(solution)/shard_map/all_to_all | solution.py:63
  839.5 13.0 %all-to-all-done.16 = bf16[16,64,256]{2,1,0:T(8,128)(2,1)S(1)} async-done(((bf16[16,64,256]{2,1,0:T(8,128)(2,1)}), bf16[16,64,256]{2,1,0:T(8,128)(2,1)S(1)}, u32[]{:S(2)}, u32[]{:S(2)}) %all-to-all-start.16) | async-done | bytes 524320 | tf_op jit(solution)/shard_map/all_to_all | solution.py:63
  856.7 16.0 %all-to-all-done.17 = bf16[16,2,64,128]{3,2,1,0:T(8,128)(2,1)S(1)} async-done(((bf16[16,2,64,128]{3,2,1,0:T(8,128)(2,1)}), bf16[16,2,64,128]{3,2,1,0:T(8,128)(2,1)S(1)}, u32[]{:S(2)}, u32[]{:S(2)}) %all-to-all-start.17) | async-done | bytes 524320 | tf_op jit(solution)/shard_map/all_to_all | solution.py:63
  (813 shorter events, 425.2 us)
Async XLA Ops:
  7.2 174.6 %all-gather.7.cloned.1.call-start = ((), (), s32[]{:S(2)}) async-start(), calls=%async_computation.22 | async-start | bytes 26738688 | tf_op jit(solution)/shard_map/all_gather | solution.py:39
  12.2 59.0 %copy-start.150 = (bf16[1,64,256]{2,1,0:T(8,128)(2,1)S(1)}, bf16[1,64,256]{2,1,0:T(8,128)(2,1)}, u32[]{:S(2)}) copy-start(bf16[1,64,256]{2,1,0:T(8,128)(2,1)} %param.14) | copy-start | bytes 98308
  70.1 349.9 %copy-start.75 = (f32[1024]{0:T(1024)}, f32[1024]{0:T(1024)S(1)}, u32[]{:S(2)}) copy-start(f32[1024]{0:T(1024)S(1)} %get-tuple-element.87) | copy-start | bytes 12292
  70.1 370.9 %copy-start.82 = (f32[1024]{0:T(1024)}, f32[1024]{0:T(1024)S(1)}, u32[]{:S(2)}) copy-start(f32[1024]{0:T(1024)S(1)} %get-tuple-element.86) | copy-start | bytes 12292
  94.2 326.0 %copy-start.5 = (bf16[1,1024,256]{2,1,0:T(8,128)(2,1)}, bf16[1,1024,256]{2,1,0:T(8,128)(2,1)S(1)}, u32[]{:S(2)}) copy-start(bf16[1,1024,256]{2,1,0:T(8,128)(2,1)S(1)} %all-gather.2) | copy-start | bytes 1572868
  120.7 302.7 %copy-start.7 = (bf16[1,256,1024]{1,2,0:T(8,128)(2,1)}, bf16[1,256,1024]{1,2,0:T(8,128)(2,1)S(1)}, u32[]{:S(2)}) copy-start(bf16[1,256,1024]{1,2,0:T(8,128)(2,1)S(1)} %all-gather.3) | copy-start | bytes 1572868
  123.1 47.0 %all-to-all-start = ((bf16[4,128,1024]{2,1,0:T(8,128)(2,1)}), bf16[4,128,1024]{2,1,0:T(8,128)(2,1)}, u32[]{:S(2)}, u32[]{:S(2)}) async-start(bf16[4,128,1024]{2,1,0:T(8,128)(2,1)} %broadcast_in_dim.130), calls=%async_computation | async-start | bytes 2097152 | tf_op jit(solution)/shard_map/all_to_all | solution.py:19
  170.1 103.9 %copy-start.125 = (s32[1024]{0:T(1024)}, s32[1024]{0:T(1024)S(1)}, u32[]{:S(2)}) copy-start(s32[1024]{0:T(1024)S(1)} %broadcast_clamp_fusion.2) | copy-start | bytes 12292
  175.8 107.4 %copy-start.67 = (f32[128,8]{1,0:T(8,128)}, f32[128,8]{1,0:T(8,128)S(1)}, u32[]{:S(2)}) copy-start(f32[128,8]{1,0:T(8,128)S(1)} %copy.441) | copy-start | bytes 12292
  287.8 18.4 %all-to-all-start.1 = ((bf16[4,128,1024]{2,1,0:T(8,128)(2,1)}), bf16[4,128,1024]{2,1,0:T(8,128)(2,1)}, u32[]{:S(2)}, u32[]{:S(2)}) async-start(bf16[4,128,1024]{2,1,0:T(8,128)(2,1)} %broadcast_in_dim.132), calls=%async_computation.1 | async-start | bytes 2097152 | tf_op jit(solution)/shard_map/all_to_all | solution.py:19
  308.6 2.8 collective-permute-start
  317.3 20.2 %all-to-all-start.2 = ((bf16[4,128,1024]{2,1,0:T(8,128)(2,1)}), bf16[4,128,1024]{2,1,0:T(8,128)(2,1)}, u32[]{:S(2)}, u32[]{:S(2)}) async-start(bf16[4,128,1024]{2,1,0:T(8,128)(2,1)} %broadcast_in_dim.135), calls=%async_computation.2 | async-start | bytes 2097152 | tf_op jit(solution)/shard_map/all_to_all | solution.py:19
  382.2 19.6 %all-to-all-start.3 = ((bf16[4,128,1024]{2,1,0:T(8,128)(2,1)}), bf16[4,128,1024]{2,1,0:T(8,128)(2,1)}, u32[]{:S(2)}, u32[]{:S(2)}) async-start(bf16[4,128,1024]{2,1,0:T(8,128)(2,1)} %broadcast_in_dim.137), calls=%async_computation.3 | async-start | bytes 2097152 | tf_op jit(solution)/shard_map/all_to_all | solution.py:19
  406.1 12.8 %collective-permute-start.1 = (bf16[128,1024]{1,0:T(8,128)(2,1)S(1)}, bf16[128,1024]{1,0:T(8,128)(2,1)}, u32[]{:S(2)}, u32[]{:S(2)}) collective-permute-start(bf16[128,1024]{1,0:T(8,128)(2,1)S(1)} %convert_element_type.522), channel_id=1, source_target_pairs={{0,64},{1,65},{2,66},{3,67},{4,68},{5,69},{6,70},{7,71},{8,72},{9,... | collective-permute-start | bytes 786440 | tf_op jit(solution)/shard_map/ppermute | solution.py:52
  424.8 15.9 %all-to-all-start.4 = ((bf16[4,128,1024]{2,1,0:T(8,128)(2,1)}), bf16[4,128,1024]{2,1,0:T(8,128)(2,1)S(1)}, u32[]{:S(2)}, u32[]{:S(2)}) async-start(bf16[4,128,1024]{2,1,0:T(8,128)(2,1)} %broadcast_in_dim.140), calls=%async_computation.4 | async-start | bytes 2097152 | tf_op jit(solution)/shard_map/all_to_all | solution.py:19
  510.9 8.5 all-to-all-start.7
  520.6 15.2 %all-to-all-start.6 = ((bf16[4,128,1024]{2,1,0:T(8,128)(2,1)}), bf16[4,128,1024]{2,1,0:T(8,128)(2,1)}, u32[]{:S(2)}, u32[]{:S(2)}) async-start(bf16[4,128,1024]{2,1,0:T(8,128)(2,1)} %broadcast_in_dim.145), calls=%async_computation.6 | async-start | bytes 2097152 | tf_op jit(solution)/shard_map/all_to_all | solution.py:19
  536.9 15.2 %all-to-all-start.5 = ((bf16[4,128,1024]{2,1,0:T(8,128)(2,1)}), bf16[4,128,1024]{2,1,0:T(8,128)(2,1)}, u32[]{:S(2)}, u32[]{:S(2)}) async-start(bf16[4,128,1024]{2,1,0:T(8,128)(2,1)} %broadcast_in_dim.142), calls=%async_computation.5 | async-start | bytes 2097152 | tf_op jit(solution)/shard_map/all_to_all | solution.py:19
  578.5 3.4 collective-permute-start.2
  585.6 42.2 %all-to-all-start.10 = ((bf16[4,128,8]{1,2,0:T(8,128)(2,1)}), bf16[4,128,8]{1,2,0:T(8,128)(2,1)S(1)}, u32[]{:S(2)}, u32[]{:S(2)}) async-start(bf16[4,128,8]{1,2,0:T(8,128)(2,1)} %broadcast_in_dim.150), calls=%async_computation.10 | async-start | bytes 16384 | tf_op jit(solution)/shard_map/all_to_all | solution.py:19
  628.9 20.1 %all-to-all-start.9 = ((bf16[4,128,1024]{2,1,0:T(8,128)(2,1)}), bf16[4,128,1024]{2,1,0:T(8,128)(2,1)}, u32[]{:S(2)}, u32[]{:S(2)}) async-start(bf16[4,128,1024]{2,1,0:T(8,128)(2,1)} %broadcast_in_dim.149), calls=%async_computation.9 | async-start | bytes 2097152 | tf_op jit(solution)/shard_map/all_to_all | solution.py:19
  633.8 268.2 %reduce-scatter.5.cloned.1.call-start = ((), (), s32[]{:S(2)}) async-start(), calls=%async_computation.24 | async-start | bytes 8912896 | tf_op jit(solution)/shard_map/reduce_scatter | solution.py:479
  676.7 3.4 collective-permute-start.3
  696.8 214.2 %reduce-scatter.3.cloned.1.call-start = ((), (), s32[]{:S(2)}) async-start(), calls=%async_computation.23 | async-start | bytes 17825792 | tf_op jit(solution)/shard_map/reduce_scatter | solution.py:476
  745.3 28.0 %all-to-all-start.13 = ((bf16[4,128,8]{1,2,0:T(8,128)(2,1)}), bf16[4,128,8]{1,2,0:T(8,128)(2,1)S(1)}, u32[]{:S(2)}, u32[]{:S(2)}) async-start(bf16[4,128,8]{1,2,0:T(8,128)(2,1)} %broadcast_in_dim.154), calls=%async_computation.13 | async-start | bytes 16384 | tf_op jit(solution)/shard_map/all_to_all | solution.py:19
  774.4 19.9 %all-to-all-start.12 = ((bf16[4,128,1024]{2,1,0:T(8,128)(2,1)}), bf16[4,128,1024]{2,1,0:T(8,128)(2,1)}, u32[]{:S(2)}, u32[]{:S(2)}) async-start(bf16[4,128,1024]{2,1,0:T(8,128)(2,1)} %broadcast_in_dim.153), calls=%async_computation.12 | async-start | bytes 2097152 | tf_op jit(solution)/shard_map/all_to_all | solution.py:19
  794.3 14.1 %all-to-all-start.19 = ((bf16[16,2,1024]{2,1,0:T(2,128)(2,1)}), bf16[16,2,1024]{2,1,0:T(2,128)(2,1)}, u32[]{:S(2)}, u32[]{:S(2)}) async-start(bf16[16,2,1024]{2,1,0:T(2,128)(2,1)} %reshape.1550), calls=%async_computation.19 | async-start | bytes 131072 | tf_op jit(solution)/shard_map/all_to_all | solution.py:63
  808.4 23.7 %all-to-all-start.18 = ((bf16[16,256,64]{1,2,0:T(8,128)(2,1)}), bf16[16,256,64]{1,2,0:T(8,128)(2,1)S(1)}, u32[]{:S(2)}, u32[]{:S(2)}) async-start(bf16[16,256,64]{1,2,0:T(8,128)(2,1)} %bitcast.214), calls=%async_computation.18 | async-start | bytes 1048576 | tf_op jit(solution)/shard_map/all_to_all | solution.py:63
  832.0 20.5 %all-to-all-start.16 = ((bf16[16,64,256]{2,1,0:T(8,128)(2,1)}), bf16[16,64,256]{2,1,0:T(8,128)(2,1)S(1)}, u32[]{:S(2)}, u32[]{:S(2)}) async-start(bf16[16,64,256]{2,1,0:T(8,128)(2,1)} %bitcast.710), calls=%async_computation.16 | async-start | bytes 1048576 | tf_op jit(solution)/shard_map/all_to_all | solution.py:63
  852.5 20.2 %all-to-all-start.17 = ((bf16[16,2,64,128]{3,2,1,0:T(8,128)(2,1)}), bf16[16,2,64,128]{3,2,1,0:T(8,128)(2,1)S(1)}, u32[]{:S(2)}, u32[]{:S(2)}) async-start(bf16[16,2,64,128]{3,2,1,0:T(8,128)(2,1)} %copy.501), calls=%async_computation.17 | async-start | bytes 1048576 | tf_op jit(solution)/shard_map/all_to_all | solution.py:63
  874.7 14.5 %all-to-all-start.14 = ((bf16[4,128,1024]{2,1,0:T(8,128)(2,1)}), bf16[4,128,1024]{2,1,0:T(8,128)(2,1)S(1)}, u32[]{:S(2)}, u32[]{:S(2)}) async-start(bf16[4,128,1024]{2,1,0:T(8,128)(2,1)} %broadcast_in_dim.155), calls=%async_computation.14 | async-start | bytes 2097152 | tf_op jit(solution)/shard_map/all_to_all | solution.py:19
  890.3 11.1 %all-to-all-start.15 = ((bf16[16,2,64]{2,1,0:T(2,128)(2,1)}), bf16[16,2,64]{2,1,0:T(2,128)(2,1)S(1)}, u32[]{:S(2)}, u32[]{:S(2)}) async-start(bf16[16,2,64]{2,1,0:T(2,128)(2,1)} %fusion.186), calls=%async_computation.15 | async-start | bytes 16384 | tf_op jit(solution)/shard_map/all_to_all | solution.py:63
  (207 other events, 2873.0 us)
Sparse Core Ops, SparseCore 0:
  12.3 168.1 all-gather.6
  697.0 82.9 reduce-scatter.4
  783.3 127.6 reduce-scatter.2
where the time goes:
time: 937 us; the launch traced here: 922 us
  local copies, waits for them, and re-layouts  252 us (27%)
  blocking collectives  153 us (16%)
  matrix products  150 us (16%)
  waiting for transfers between devices  143 us (15%)
  other arithmetic  122 us (13%)
  starting transfers between devices  83 us (9%)
  between operations  17.6 us (2%)
    all_to_all x13, waiting for transfers between devices, from_everyone(): return lax.all_to_all(copies, axis, split_axis=0, concat_axis=0, tiled=True)  82.9 us
    split x4, local copies, waits for them, and re-layouts, rows_first(): jnp.split(result, [sum(widths[:k]) for k in range(1, len(widths))], axis=1)  56.1 us
    all_to_all x13, starting transfers between devices, from_everyone(): return lax.all_to_all(copies, axis, split_axis=0, concat_axis=0, tiled=True)  53.6 us
    all_to_all x5, waiting for transfers between devices, sent_and_summed(): lax.all_to_all(tiles, axis, split_axis=0, concat_axis=0, tiled=True)  49.2 us
    dot_general x3, matrix products, expert_apply(): jnp.einsum('ecd,sedf->secf', expert_in, w_gateup, preferred_element_type=...  35.6 us
    another operation x24, other arithmetic  34 us
    all_to_all x2, blocking collectives, from_everyone(): return lax.all_to_all(copies, axis, split_axis=0, concat_axis=0, tiled=True)  30.1 us
    dot_general x3, matrix products, expert_grad_apply(): jnp.einsum('secf,sedf->ecd', gate_up_grad, w_gateup, preferred_element_ty...  28.3 us
  transfers between devices with their start and end apart: 25, of which 18 were waited for; matrix products, arithmetic and copies ran while one was open for 24% of the time, Pallas kernels for 0%

commit v1 on v0

v1 whole, which is shorter than its diff:
```python
import jax
import jax.numpy as jnp
from jax import lax
from jax.experimental import pallas as pl
from jax.experimental.pallas import tpu as pltpu
from jax.sharding import PartitionSpec as P

HEAD_SIZE = 64
E = 32
TOPK = 8
CAP = 48
ROWS = 128
WIDTH = 1024
FF = 512
PART = 32
LOCAL = 8
DENSE = 896

epsilon = 1e-06
rope_base = 10000.0
masked_score = -1e30
f32 = jnp.float32
bf16 = jnp.bfloat16
MESH = pl.DeviceIdType.MESH


def dot(a, b):
    return lax.dot_general(a, b, (((1,), (0,)), ((), ())), preferred_element_type=f32)


def dot_nt(a, b):
    return lax.dot_general(a, b, (((1,), (1,)), ((), ())), preferred_element_type=f32)


def dot_tn(a, b):
    return lax.dot_general(a, b, (((0,), (0,)), ((), ())), preferred_element_type=f32)


def scale_of(values):
    return lax.rsqrt(jnp.mean(values * values, axis=1, keepdims=True) + epsilon)


def norm_back(values, gain_row, upstream):
    scale = scale_of(values)
    weighted = upstream * gain_row
    inner = jnp.mean(weighted * values, axis=1, keepdims=True)
    back = scale * weighted - values * (scale * scale * scale * inner)
    return back, jnp.sum(upstream * values * scale, axis=0, keepdims=True)


def low_lanes():
    return lax.broadcasted_iota(jnp.int32, (ROWS, 128), 1) < 64


def turn(chunk, cos, sin):
    place = lax.broadcasted_iota(jnp.int32, (ROWS, 128), 1) % 64
    swapped = jnp.where(place < 32, pltpu.roll(chunk, 96, 1), pltpu.roll(chunk, 32, 1))
    return chunk * cos + swapped * sin


def doubled(both):
    wide = both.astype(f32)
    other = pltpu.roll(wide, 64, 1)
    left = low_lanes()
    return (
        jnp.where(left, wide, other).astype(bf16),
        jnp.where(left, other, wide).astype(bf16),
    )


def half(chunk, which):
    left = low_lanes()
    keep = left if which == 0 else jnp.logical_not(left)
    return jnp.where(keep, chunk, jnp.zeros_like(chunk))


def soft(query_half, keys, seen):
    scores = dot_nt(query_half, keys) * HEAD_SIZE ** (-0.5)
    scores = jnp.where(seen, scores, masked_score)
    raised = jnp.exp(scores - jnp.max(scores, axis=1, keepdims=True))
    return raised / jnp.sum(raised, axis=1, keepdims=True)


def body(
    dense, experts, first_x, cotangent, routes, cos_ref, sin_ref, seen_ref,
    out_ref, grad_ref, dense_grad, expert_grad,
    xin, uin, turned, first_in, qkv, mixed, middle, chosen, chance, slot_gate,
    rs_send, rs_recv, ag, small, slots, packed, x_rows, og_rows, gate_s, up_s, hid_s,
    y_rows, ret, gg_low, ug_low, gate_grads, resid, gains, router_back, dqkv, swap_out, swap_in,
    rs_ss, rs_rs, ag_ss, ag_rs, sm_ss, sm_rs, d_ss, d_rs, r_ss, r_rs, w_ss, w_rs,
):
    s = lax.axis_index("section")
    x = lax.axis_index("tensor")
    d = lax.axis_index("dp")
    z, y = d // 4, d % 4
    zz = z % 2
    mine = zz * 4 + y
    rows_mine = pl.ds(pl.multiple_of(x * PART, PART), PART)
    experts_mine = pl.ds(pl.multiple_of(x * LOCAL, LOCAL), LOCAL)
    near = [(kz, ky) for kz in range(2) for ky in range(4)]

    def spot(kz, ky):
        z2, y2 = (zz + kz) % 2, (y + ky) % 4
        return z2 * 4 + y2, ((z // 2) * 2 + z2) * 4 + y2

    barrier = pltpu.get_barrier_semaphore()
    for k in range(1, 4):
        pl.semaphore_signal(
            barrier, inc=1, device_id={"tensor": (x + k) % 4}, device_id_type=MESH
        )
    for kz, ky in near:
        peer = spot(kz, ky)[1]
        if (kz, ky) != (0, 0):
            pl.semaphore_signal(barrier, inc=1, device_id={"dp": peer}, device_id_type=MESH)
        pl.semaphore_signal(
            barrier, inc=1, device_id={"section": 1 - s, "dp": peer}, device_id_type=MESH
        )
    pl.semaphore_wait(barrier, 18)

    def remote(src, dst, send, recv, device):
        return pltpu.make_async_remote_copy(
            src_ref=src, dst_ref=dst, send_sem=send, recv_sem=recv,
            device_id=device, device_id_type=MESH,
        )

    def scatter_copies(l, j):
        copies = []
        for k in range(1, 4):
            p = (x + k) % 4
            src = rs_send.at[l, j, pl.ds(pl.multiple_of(p * PART, PART), PART)]
            copies.append(
                remote(src, rs_recv.at[l, j, k - 1], rs_ss.at[l, j, k - 1],
                       rs_rs.at[l, j, k - 1], {"tensor": p})
            )
        return copies

    def scatter_start(l, j, partial):
        rs_send[l, j] = partial.astype(bf16)
        for copy in scatter_copies(l, j):
            copy.start()

    def scatter_end(l, j):
        for copy in scatter_copies(l, j):
            copy.wait()
        total = rs_send[l, j, rows_mine].astype(f32)
        for k in range(3):
            total = total + rs_recv[l, j, k].astype(f32)
        return total

    def gather_copies(l, j):
        copies = []
        for k in range(1, 4):
            ref = ag.at[l, j, rows_mine]
            copies.append(
                remote(ref, ref, ag_ss.at[l, j, k - 1], ag_rs.at[l, j, k - 1],
                       {"tensor": (x + k) % 4})
            )
        return copies

    def gather_start(l, j, rows):
        ag[l, j, rows_mine] = rows.astype(bf16)
        for copy in gather_copies(l, j):
            copy.start()

    def gather_end(l, j):
        for copy in gather_copies(l, j):
            copy.wait()

    def small_copies(l, j):
        copies = []
        for k in range(1, 4):
            ref = small.at[l, j, x]
            copies.append(
                remote(ref, ref, sm_ss.at[l, j, k - 1], sm_rs.at[l, j, k - 1],
                       {"tensor": (x + k) % 4})
            )
        return copies

    def block(index):
        return pl.ds(pl.multiple_of(index * CAP, CAP), CAP)

    def dispatch_copies(l, way, act):
        rel = (s + l) % 2
        target = x_rows if way == 0 else og_rows
        for kz, ky in near:
            i, peer = spot(kz, ky)
            n = kz * 4 + ky
            src = packed.at[l, way, block(i)]
            dst = target.at[block(rel * 8 + mine)]
            far = remote(src, dst, d_ss.at[l, way, n], d_rs.at[way, rel * 8 + n],
                         {"section": l, "dp": peer})
            if n == 0:
                @pl.when(s == l)
                def _():
                    if act == 0:
                        pltpu.make_async_copy(src, dst, d_rs.at[way, 0]).start()

                @pl.when(s != l)
                def _():
                    if act == 0:
                        far.start()
                    else:
                        far.wait_send()
            elif act == 0:
                far.start()
            else:
                far.wait_send()

    def dispatch_arrived(way, rel):
        target = x_rows if way == 0 else og_rows
        for n in range(8):
            dst = target.at[block(rel * 8 + n)]
            src = packed.at[0, way, block(n)]
            if rel == 0 and n == 0:
                pltpu.make_async_copy(
                    packed.at[0, way, block(mine)], target.at[block(mine)], d_rs.at[way, 0]
                ).wait()
            else:
                remote(src, dst, d_ss.at[0, way, n], d_rs.at[way, rel * 8 + n],
                       {"dp": spot(0, 1)[1]}).wait_recv()

    def return_copies(l, way, rel, act):
        for kz, ky in near:
            i, peer = spot(kz, ky)
            n = kz * 4 + ky
            src = y_rows.at[way, block(rel * 8 + i)]
            dst = ret.at[l, way, block(mine)]
            if rel == 0 and n == 0:
                if act == 0:
                    pltpu.make_async_copy(src, dst, r_rs.at[l, way, 0]).start()
                continue
            far = remote(src, dst, r_ss.at[way, rel * 8 + n], r_rs.at[l, way, n],
                         {"section": (s + rel) % 2, "dp": peer})
            if act == 0:
                far.start()
            else:
                far.wait_send()

    def return_arrived(l, way):
        for kz, ky in near:
            i, peer = spot(kz, ky)
            n = kz * 4 + ky
            src = y_rows.at[way, block(n)]
            dst = ret.at[l, way, block(i)]
            far = remote(src, dst, r_ss.at[way, n], r_rs.at[l, way, n],
                         {"section": 1 - s, "dp": peer})
            if n == 0:
                @pl.when(s == l)
                def _():
                    pltpu.make_async_copy(src, dst, r_rs.at[l, way, 0]).wait()

                @pl.when(s != l)
                def _():
                    far.wait_recv()
            else:
                far.wait_recv()

    def swap_copy(way):
        return remote(swap_out.at[way], swap_in.at[way], w_ss.at[way], w_rs.at[way],
                      {"section": 1 - s})

    def keep_result(way, l, ref):
        @pl.when(s == l)
        def _():
            ref[s] = ag[l, 1 + 2 * way].astype(f32)

        @pl.when(s != l)
        def _():
            swap_out[way] = ag[l, 1 + 2 * way]
            swap_copy(way).start()

    xin[0] = first_x[...]
    uin[1] = cotangent[...]

    def forward(l, carry):
        turned[l] = dense[l, :, 768:896].astype(f32).T
        values = xin[l]
        first = (values * scale_of(values) * turned[l, 32:33]).astype(bf16)
        first_in[l] = first
        made = dot(first, dense[l, :, 0:512])
        cos, sin = cos_ref[...], sin_ref[...]
        for c in range(3):
            cut = slice(128 * c, 128 * c + 128)
            qkv[l, :, cut] = turn(made[:, cut], cos, sin).astype(bf16)
        qkv[l, :, 384:512] = made[:, 384:512].astype(bf16)
        seen = seen_ref[...] > 0
        keys = doubled(qkv[l, :, 256:384])
        vals = doubled(qkv[l, :, 384:512])
        for c in range(2):
            cut = slice(128 * c, 128 * c + 128)
            query = qkv[l, :, cut]
            got = [
                dot(soft(half(query, b), keys[c], seen).astype(bf16), vals[c]) for b in range(2)
            ]
            mixed[l, :, cut] = jnp.where(low_lanes(), got[0], got[1]).astype(bf16)
        scatter_start(l, 0, dot_nt(mixed[l], dense[l, :, 512:768]))

        experts_iota = lax.broadcasted_iota(jnp.int32, (E, ROWS), 0)
        named = jnp.zeros((E, ROWS), f32)
        for k in range(TOPK):
            named = named + (experts_iota == routes[l, k:k + 1]).astype(f32)
        before = (
            lax.broadcasted_iota(jnp.int32, (ROWS, ROWS), 0)
            < lax.broadcasted_iota(jnp.int32, (ROWS, ROWS), 1)
        ).astype(bf16)
        place = dot(named.astype(bf16), before)
        slots[...] = jnp.where(named > 0, place, -1.0)
        place = slots[experts_mine]
        slot_iota = lax.broadcasted_iota(jnp.int32, (CAP, ROWS), 0).astype(f32)
        for i in range(LOCAL):
            chosen[l, CAP * i:CAP * i + CAP] = (slot_iota == place[i:i + 1]).astype(bf16)

        center = xin[l, rows_mine] + scatter_end(l, 0)
        middle[l] = center
        gather_start(l, 0, center * scale_of(center) * turned[l, 33:34])
        gather_end(l, 0)

        second = ag[l, 0]
        packed[l, 0] = dot(chosen[l], second).astype(bf16)
        dispatch_copies(l, 0, 0)
        logits = dot_nt(turned[l, 0:32].astype(bf16), second)
        logits = jnp.where(named > 0, logits, masked_score)
        raised = jnp.where(named > 0, jnp.exp(logits - jnp.max(logits, axis=0, keepdims=True)), 0.0)
        chance[l] = raised / jnp.sum(raised, axis=0, keepdims=True)
        gate = chance[l, experts_mine]
        for i in range(LOCAL):
            cut = slice(CAP * i, CAP * i + CAP)
            weighted = chosen[l, cut].astype(f32) * gate[i:i + 1]
            slot_gate[l, cut] = jnp.sum(weighted, axis=1, keepdims=True)

        @pl.when(s == l)
        def _():
            for rel in range(2):
                dispatch_arrived(0, rel)
                cut = slice(384 * rel, 384 * rel + 384)
                rows = x_rows[cut]
                gate_part = dot(rows, experts[0])
                up_part = dot(rows, experts[1])
                gate_s[cut] = gate_part
                up_s[cut] = up_part
                hidden = (gate_part / (1.0 + jnp.exp(-gate_part)) * up_part).astype(bf16)
                hid_s[cut] = hidden
                y_rows[0, cut] = dot_nt(hidden, experts[2]).astype(bf16)
                return_copies(l, 0, rel, 0)

        return_arrived(l, 0)
        scaled = ret[l, 0].astype(f32) * slot_gate[l]
        scatter_start(l, 1, dot_tn(chosen[l], scaled.astype(bf16)))
        gather_start(l, 1, middle[l] + scatter_end(l, 1))
        gather_end(l, 1)
        xin[l + 1] = ag[l, 1].astype(f32)
        keep_result(0, l, out_ref)
        dispatch_copies(l, 0, 1)
        return carry

    lax.fori_loop(0, 2, forward, 0)

    def backward(step, carry):
        l = 1 - step
        upstream = uin[l].astype(bf16)
        spread = dot(chosen[l], upstream)
        packed[l, 1] = (spread * slot_gate[l]).astype(bf16)
        dispatch_copies(l, 1, 0)
        inner = jnp.sum(spread * ret[l, 0].astype(f32), axis=1, keepdims=True)
        for i in range(LOCAL):
            cut = slice(CAP * i, CAP * i + CAP)
            row = jnp.sum(chosen[l, cut].astype(f32) * inner[cut], axis=0, keepdims=True)
            gate_grads[i:i + 1] = row
        small[l, 0, x, 0:8] = gate_grads[...]
        for copy in small_copies(l, 0):
            copy.start()

        @pl.when(s == l)
        def _():
            for rel in range(2):
                dispatch_arrived(1, rel)
                cut = slice(384 * rel, 384 * rel + 384)
                hidden_grad = dot(og_rows[cut], experts[2])
                gate_part = gate_s[cut]
                up_part = up_s[cut]
                sig = 1.0 / (1.0 + jnp.exp(-gate_part))
                gate_low = (
                    hidden_grad * up_part * sig * (1.0 + gate_part * (1.0 - sig))
                ).astype(bf16)
                up_low = (hidden_grad * gate_part * sig).astype(bf16)
                gg_low[cut] = gate_low
                ug_low[cut] = up_low
                back = dot_nt(gate_low, experts[0]) + dot_nt(up_low, experts[1])
                y_rows[1, cut] = back.astype(bf16)
                return_copies(l, 1, rel, 0)
            expert_grad[0] = dot_tn(x_rows[...], gg_low[...]).astype(bf16)
            expert_grad[1] = dot_tn(x_rows[...], ug_low[...]).astype(bf16)
            expert_grad[2] = dot_tn(og_rows[...], hid_s[...]).astype(bf16)

        for copy in small_copies(l, 0):
            copy.wait()
        gate = chance[l]
        gate_total = jnp.concatenate([small[l, 0, p, 0:8] for p in range(4)], axis=0)
        picked = gate * (gate_total - jnp.sum(gate * gate_total, axis=0, keepdims=True))
        logit_low = picked.astype(bf16)
        router_back[...] = dot_tn(logit_low, turned[l, 0:32].astype(bf16))
        return_arrived(l, 1)
        scatter_start(l, 2, dot_tn(chosen[l], ret[l, 1]))
        router_grad = dot(logit_low, ag[l, 0])
        arrived = scatter_end(l, 2) + router_back[rows_mine]
        back, gain_two = norm_back(middle[l], turned[l, 33:34], arrived)
        kept = uin[l, rows_mine] + back
        resid[...] = kept
        gather_start(l, 2, kept)
        gather_end(l, 2)

        branch = ag[l, 2]
        mixed_grad = dot(branch, dense[l, :, 512:768]).astype(bf16)
        seen = seen_ref[...] > 0
        cos, sin = cos_ref[...], -sin_ref[...]
        left = low_lanes()
        keys = doubled(qkv[l, :, 256:384])
        vals = doubled(qkv[l, :, 384:512])
        key_grads, value_grads = [], []
        for c in range(2):
            cut = slice(128 * c, 128 * c + 128)
            query, above = qkv[l, :, cut], mixed_grad[:, cut]
            parts, key_grad, value_grad = [], 0.0, 0.0
            for b in range(2):
                query_half, above_half = half(query, b), half(above, b)
                prob = soft(query_half, keys[c], seen)
                value_grad = value_grad + dot_tn(prob.astype(bf16), above_half)
                prob_grad = dot_nt(above_half, vals[c])
                mean = jnp.sum(prob * prob_grad, axis=1, keepdims=True)
                score_low = (prob * (prob_grad - mean)).astype(bf16)
                parts.append(dot(score_low, keys[c]))
                key_grad = key_grad + dot_tn(score_low, query_half)
            query_grad = jnp.where(left, parts[0], parts[1]) * HEAD_SIZE ** (-0.5)
            dqkv[:, cut] = turn(query_grad, cos, sin).astype(bf16)
            key_grads.append(key_grad + pltpu.roll(key_grad, 64, 1))
            value_grads.append(value_grad + pltpu.roll(value_grad, 64, 1))
        key_grad = jnp.where(left, key_grads[0], key_grads[1]) * HEAD_SIZE ** (-0.5)
        dqkv[:, 256:384] = turn(key_grad, cos, sin).astype(bf16)
        dqkv[:, 384:512] = jnp.where(left, value_grads[0], value_grads[1]).astype(bf16)
        scatter_start(l, 3, dot_nt(dqkv[...], dense[l, :, 0:512]))
        dense_grad[l, :, 0:512] = dot_tn(first_in[l], dqkv[...]).astype(bf16)
        dense_grad[l, :, 512:768] = dot_tn(branch, mixed[l]).astype(bf16)
        back, gain_one = norm_back(xin[l, rows_mine], turned[l, 32:33], scatter_end(l, 3))
        gather_start(l, 3, resid[...] + back)
        gains[l, x, 0:1] = gain_one
        gains[l, x, 1:2] = gain_two
        for k in range(1, 4):
            ref = gains.at[l, x]
            remote(ref, ref, sm_ss.at[l, 1, k - 1], sm_rs.at[l, 1, k - 1],
                   {"tensor": (x + k) % 4}).start()
        gather_end(l, 3)
        uin[1 - l] = ag[l, 3].astype(f32)
        keep_result(1, l, grad_ref)
        for k in range(1, 4):
            ref = gains.at[l, x]
            remote(ref, ref, sm_ss.at[l, 1, k - 1], sm_rs.at[l, 1, k - 1],
                   {"tensor": (x + k) % 4}).wait()
        total = gains[l, 0] + gains[l, 1] + gains[l, 2] + gains[l, 3]
        last = jnp.concatenate([router_grad, total, jnp.zeros((88, WIDTH), f32)], axis=0)
        dense_grad[l, :, 768:896] = last.T.astype(bf16)
        dispatch_copies(l, 1, 1)
        return carry

    lax.fori_loop(0, 2, backward, 0)

    for way, ref in ((0, out_ref), (1, grad_ref)):
        swap_copy(way).wait()
        ref[1 - s] = swap_in[way].astype(f32)
        for rel in range(2):
            return_copies(s, way, rel, 1)


def layers(*operands):
    shape = jax.ShapeDtypeStruct
    scratch = [
        pltpu.VMEM((3, ROWS, WIDTH), f32),
        pltpu.VMEM((2, ROWS, WIDTH), f32),
        pltpu.VMEM((2, ROWS, WIDTH), f32),
        pltpu.VMEM((2, ROWS, WIDTH), bf16),
        pltpu.VMEM((2, ROWS, 512), bf16),
        pltpu.VMEM((2, ROWS, 256), bf16),
        pltpu.VMEM((2, PART, WIDTH), f32),
        pltpu.VMEM((2, LOCAL * CAP, ROWS), bf16),
        pltpu.VMEM((2, E, ROWS), f32),
        pltpu.VMEM((2, LOCAL * CAP, 1), f32),
        pltpu.VMEM((2, 4, ROWS, WIDTH), bf16),
        pltpu.VMEM((2, 4, 3, PART, WIDTH), bf16),
        pltpu.VMEM((2, 4, ROWS, WIDTH), bf16),
        pltpu.VMEM((2, 1, 4, 8, ROWS), f32),
        pltpu.VMEM((E, ROWS), f32),
        pltpu.VMEM((2, 2, LOCAL * CAP, WIDTH), bf16),
        pltpu.VMEM((2 * LOCAL * CAP, WIDTH), bf16),
        pltpu.VMEM((2 * LOCAL * CAP, WIDTH), bf16),
        pltpu.VMEM((2 * LOCAL * CAP, FF), f32),
        pltpu.VMEM((2 * LOCAL * CAP, FF), f32),
        pltpu.VMEM((2 * LOCAL * CAP, FF), bf16),
        pltpu.VMEM((2, 2 * LOCAL * CAP, WIDTH), bf16),
        pltpu.VMEM((2, 2, LOCAL * CAP, WIDTH), bf16),
        pltpu.VMEM((2 * LOCAL * CAP, FF), bf16),
        pltpu.VMEM((2 * LOCAL * CAP, FF), bf16),
        pltpu.VMEM((8, ROWS), f32),
        pltpu.VMEM((PART, WIDTH), f32),
        pltpu.VMEM((2, 4, 8, WIDTH), f32),
        pltpu.VMEM((ROWS, WIDTH), f32),
        pltpu.VMEM((ROWS, 512), bf16),
        pltpu.VMEM((2, ROWS, WIDTH), bf16),
        pltpu.VMEM((2, ROWS, WIDTH), bf16),
        pltpu.SemaphoreType.DMA((2, 4, 3)),
        pltpu.SemaphoreType.DMA((2, 4, 3)),
        pltpu.SemaphoreType.DMA((2, 4, 3)),
        pltpu.SemaphoreType.DMA((2, 4, 3)),
        pltpu.SemaphoreType.DMA((2, 2, 3)),
        pltpu.SemaphoreType.DMA((2, 2, 3)),
        pltpu.SemaphoreType.DMA((2, 2, 8)),
        pltpu.SemaphoreType.DMA((2, 16)),
        pltpu.SemaphoreType.DMA((2, 16)),
        pltpu.SemaphoreType.DMA((2, 2, 8)),
        pltpu.SemaphoreType.DMA((2,)),
        pltpu.SemaphoreType.DMA((2,)),
    ]
    return pl.pallas_call(
        body,
        out_shape=(
            shape((2, ROWS, WIDTH), f32),
            shape((2, ROWS, WIDTH), f32),
            shape((2, WIDTH, DENSE), bf16),
            shape((3, WIDTH, FF), bf16),
        ),
        in_specs=[pl.BlockSpec(memory_space=pltpu.VMEM)] * 8,
        out_specs=tuple(pl.BlockSpec(memory_space=pltpu.VMEM) for _ in range(4)),
        scratch_shapes=scratch,
        compiler_params=pltpu.CompilerParams(
            collective_id=0, has_side_effects=True, vmem_limit_bytes=60 * 1024 * 1024
        ),
        name="layers",
    )(*operands)


def doc_tables(lengths):
    doc_ends = jnp.cumsum(lengths)
    doc_starts = doc_ends - lengths
    places = jnp.arange(ROWS, dtype=jnp.int32)
    segment = jnp.sum((places[:, None] >= doc_ends[None, :]).astype(jnp.int32), axis=1)
    owners = segment[:, None] == jnp.arange(lengths.shape[0], dtype=jnp.int32)[None, :]
    offset = places - jnp.sum(jnp.where(owners, doc_starts[None, :], 0), axis=1)
    visible = (segment[:, None] == segment[None, :]) & (places[None, :] <= places[:, None])
    half_dim = HEAD_SIZE // 2
    frequency = rope_base ** (-2.0 * jnp.arange(half_dim, dtype=f32) / HEAD_SIZE)
    angles = offset.astype(f32)[:, None] * frequency[None, :]
    cos, sin = jnp.cos(angles), jnp.sin(angles)
    return (
        jnp.concatenate([cos] * 4, axis=1),
        jnp.concatenate([-sin, sin, -sin, sin], axis=1),
        visible.astype(f32),
    )


def local(
    boundary,
    doc_lengths,
    routes,
    norm_gains,
    w_query,
    key_value_weight,
    w_out,
    w_router,
    w_gateup,
    w_down,
):
    s = lax.axis_index("section")
    low = s == 0
    swap = [(0, 1), (1, 0)]

    def exchanged(pair):
        own = jnp.where(low, pair[0], pair[1])
        sent = jnp.where(low, pair[1], pair[0])
        got = lax.ppermute(sent, "section", swap)
        return jnp.where(low, own, got), jnp.where(low, got, own)

    first_x, cotangent = exchanged(boundary[0])
    routes_here = jnp.stack(exchanged(jnp.swapaxes(routes[0], 1, 2)))
    cos, sin, seen = doc_tables(jnp.where(low, doc_lengths[0, 0], doc_lengths[1, 0]))

    depth = w_query.shape[1]
    piece = jnp.concatenate(
        [
            w_query[0],
            key_value_weight[0, 0],
            key_value_weight[0, 1],
            w_out[0].T,
            w_router[0],
            norm_gains[0].T,
            jnp.zeros((depth, DENSE - 802), bf16),
        ],
        axis=1,
    )
    dense = lax.all_gather(piece, ("section", "dp"), axis=0, tiled=True)
    dense = dense.reshape(2, WIDTH, DENSE)

    own = jnp.concatenate(
        [jnp.swapaxes(w_gateup[0], 0, 1), jnp.swapaxes(w_down[0], 1, 2)[:, None]], axis=1
    )
    own = own.reshape(4, 1, 2, 4, 3, 64, 128)
    own = jnp.broadcast_to(own, (4, 2, 2, 4, 3, 64, 128)).reshape(64, 3, 64, 128)
    arrived = lax.all_to_all(own, ("tensor", "dp"), split_axis=0, concat_axis=0, tiled=True)
    experts = arrived.reshape(4, 16, 3, 64, 128).transpose(2, 1, 3, 0, 4).reshape(3, WIDTH, FF)

    outs, grads, dense_grad, expert_grad = layers(
        dense, experts, first_x, cotangent, routes_here, cos, sin, seen
    )

    parts = lax.all_to_all(
        dense_grad.reshape(32, 64, DENSE), ("section", "dp"), split_axis=0, concat_axis=0, tiled=True
    )
    parts = jnp.sum(parts.astype(f32), axis=0)
    pieces = expert_grad.reshape(3, 16, 64, 4, 128).transpose(3, 1, 0, 2, 4).reshape(64, 3, 64, 128)
    pieces = lax.all_to_all(pieces, ("tensor", "dp"), split_axis=0, concat_axis=0, tiled=True)
    pieces = jnp.sum(pieces.reshape(4, 2, 8, 3, 64, 128).astype(f32), axis=1)
    pieces = pieces.reshape(E, 3, 64, 128)
    return (
        outs[None],
        grads[None],
        parts[:, 800:802].T[None],
        parts[:, 0:256][None],
        jnp.stack([parts[:, 256:384], parts[:, 384:512]])[None],
        parts[:, 512:768].T[None],
        parts[:, 768:800][None],
        jnp.swapaxes(pieces[:, 0:2], 0, 1)[None],
        jnp.swapaxes(pieces[:, 2], 1, 2)[None],
    )


def solution(mesh):
    placed = (
        P("section", None, "dp", None),
        P(None, "dp", None),
        P("section", None, "dp", None),
        P("section", None, "dp"),
        P("section", "dp", "tensor"),
        P("section", None, "dp", "tensor"),
        P("section", "tensor", "dp"),
        P("section", "dp", None),
        P("section", None, None, "dp", "tensor"),
        P("section", None, "tensor", "dp"),
    )
    return jax.shard_map(
        local,
        mesh=mesh,
        in_specs=placed,
        out_specs=(
            P("section", None, "dp", None),
            P("section", None, "dp", None),
            P("section", None, "dp"),
            P("section", "dp", "tensor"),
            P("section", None, "dp", "tensor"),
            P("section", "tensor", "dp"),
            P("section", "dp", None),
            P("section", None, None, "dp", "tensor"),
            P("section", None, "tensor", "dp"),
        ),
        check_vma=False,
    )
```

time: 937 us -> 407 us (0.43); the launches traced: 922 us -> 405 us
  local copies, waits for them, and re-layouts: 252 us -> 28.3 us
  Pallas kernels: 0 us -> 195 us
  matrix products: 150 us -> 0 us
  other arithmetic: 122 us -> 12.8 us
  blocking collectives: 153 us -> 47.8 us
  starting transfers between devices: 83 us -> 17.1 us
  waiting for transfers between devices: 143 us -> 90.1 us
    pallas_call x0 -> x1, Pallas kernels: none -> 195 us  [layers(): pl.pallas_call(body, out_shape=(shape((2, ROWS, WIDTH), f32), shape((2, R...]
    dot_general x57 -> x0, matrix products: 149 us -> none  [the longest x3 35.6 us: expert_apply(): jnp.einsum('ecd,sedf->secf', expert_in, w_gateup, preferred_element_type=...]
    all_gather x5 -> x0, blocking collectives: 123 us -> none  [the longest x1 26.5 us: local(): lax.all_gather(key_value_weight[0], 'dp', axis=1, tiled=True)]
    gather x12 -> x0, local copies, waits for them, and re-layouts: 90.8 us -> none  [the longest x3 27.8 us: layer_forward(): expert_out.reshape(E * CAP, -1)[pair_slot].reshape(count_of_rows, TOPK, -1)]
    all_to_all x18 -> x2, starting transfers between devices: 76 us -> 16.5 us  [the longest x1 11.6 us: local(): lax.all_to_all(own, ('tensor', 'dp'), split_axis=0, concat_axis=0, tiled=...]
    split x4 -> x0, local copies, waits for them, and re-layouts: 56.1 us -> none  [rows_first(): jnp.split(result, [sum(widths[:k]) for k in range(1, len(widths))], axis=1)]
    all_to_all x18 -> x2, waiting for transfers between devices: 132 us -> 79.6 us  [the longest x1 45.4 us: local(): lax.all_to_all(dense_grad.reshape(32, 64, DENSE), ('section', 'dp'), spli...]
    reduce_sum x60 -> x4, other arithmetic: 52.3 us -> 3.46 us  [the longest x1 2.57 us: local(): parts = jnp.sum(parts.astype(f32), axis=0)]
  transfers between devices with their start and end apart: 25 -> 5, of which waited for: 18 -> 3; matrix products, arithmetic and copies ran while one was open for 24% -> 6% of each run, Pallas kernels for 0% -> 0%
where the time goes in v1:
time: 407 us; the launch traced here: 405 us
  Pallas kernels  195 us (48%)
  waiting for transfers between devices  90.1 us (22%)
  blocking collectives  47.8 us (12%)
  local copies, waits for them, and re-layouts  28.3 us (7%)
  starting transfers between devices  17.1 us (4%)
  between operations  14.2 us (3%)
  other arithmetic  12.8 us (3%)
    pallas_call x1, Pallas kernels, layers(): pl.pallas_call(body, out_shape=(shape((2, ROWS, WIDTH), f32), shape((2, R...  195 us
    all_to_all x1, blocking collectives, local(): lax.all_to_all(pieces, ('tensor', 'dp'), split_axis=0, concat_axis=0, til...  47.8 us
    all_to_all x1, waiting for transfers between devices, local(): lax.all_to_all(dense_grad.reshape(32, 64, DENSE), ('section', 'dp'), spli...  45.4 us
    all_to_all x1, waiting for transfers between devices, local(): lax.all_to_all(own, ('tensor', 'dp'), split_axis=0, concat_axis=0, tiled=...  34.2 us
    all_to_all x1, starting transfers between devices, local(): lax.all_to_all(own, ('tensor', 'dp'), split_axis=0, concat_axis=0, tiled=...  11.6 us
    all_gather x1, waiting for transfers between devices, local(): dense = lax.all_gather(piece, ('section', 'dp'), axis=0, tiled=True)  10.5 us
  transfers between devices with their start and end apart: 5, of which 3 were waited for; matrix products, arithmetic and copies ran while one was open for 6% of the time, Pallas kernels for 0%

profile of v1, /device:TPU:0, one launch (start us, length us, event | category | flops | bytes accessed | tf_op | source)
XLA Modules:
  0.0 405.0 jit_solution(15209830575752262768)
XLA Ops:
  7.2 0.8 copy.48
  8.0 0.8 copy.47
  8.8 0.7 slice_bitcast_fusion.7
  9.5 1.5 concatenate.17
  11.1 1.5 maximum_bitcast_fusion
  12.8 2.6 broadcast_in_dim.63
  15.4 11.6 %all-to-all-start = ((bf16[64,3,64,128]{3,2,1,0:T(8,128)(2,1)}), bf16[64,3,64,128]{3,2,1,0:T(8,128)(2,1)S(1)}, u32[]{:S(2)}, u32[]{:S(2)}) async-start(bf16[64,3,64,128]{3,2,1,0:T(8,128)(2,1)} %bitcast.95), calls=%async_computation | async-start | bytes 6291456 | tf_op jit(solution)/shard_map/all_to_all | solution.py:605
  27.1 2.1 select_bitcast_fusion
  30.4 0.7 fusion.1.seen_ref
  31.1 0.8 pad_maximum_fusion
  32.0 0.6 pad_add_fusion.routes
  32.6 2.5 bitcast_select_fusion
  35.0 34.2 %all-to-all-done = bf16[64,3,64,128]{3,2,1,0:T(8,128)(2,1)S(1)} async-done(((bf16[64,3,64,128]{3,2,1,0:T(8,128)(2,1)}), bf16[64,3,64,128]{3,2,1,0:T(8,128)(2,1)S(1)}, u32[]{:S(2)}, u32[]{:S(2)}) %all-to-all-start) | async-done | bytes 3145760 | tf_op jit(solution)/shard_map/all_to_all | solution.py:605
  69.2 4.7 %copy.50 = bf16[3,16,64,4,128]{4,3,2,1,0:T(4,128)(2,1)} copy(bf16[3,16,64,4,128]{4,2,0,1,3:T(8,128)(2,1)S(1)} %bitcast.94) | data formatting | bytes 6291456 | tf_op jit(solution)/shard_map/transpose | solution.py:606
  73.9 5.7 %reshape.127.experts = bf16[3,1024,512]{2,1,0:T(8,128)(2,1)} reshape(bf16[3,16,64,4,128]{4,3,2,1,0:T(4,128)(2,1)} %copy.50) | data formatting | bytes 6291456 | tf_op jit(solution)/shard_map/reshape | solution.py:606
  79.7 10.5 %all-gather.2.cloned.1.call-done = bf16[2048,896]{1,0:T(8,128)(2,1)} async-done(((bf16[64,896]{1,0:T(8,128)(2,1)}), bf16[2048,896]{1,0:T(8,128)(2,1)}) %all-gather.2.cloned.1.call-update) | async-done | bytes 3670032 | tf_op jit(solution)/shard_map/all_gather | solution.py:597
  90.2 194.7 %layers.1 = (f32[2,128,1024]{2,1,0:T(8,128)}, f32[2,128,1024]{2,1,0:T(8,128)}, bf16[2,1024,896]{2,1,0:T(8,128)(2,1)}, bf16[3,1024,512]{2,1,0:T(8,128)(2,1)}) custom-call(bf16[2,1024,896]{2,1,0:T(8,128)(2,1)} %bitcast.100, bf16[3,1024,512]{2,1,0:T(8,128)(2,1)} %reshape.127.experts, f32[128,1024]{1,0:T(8,128)} %get-tuple-element.54.first_x, ...), custom_call_target="tpu_custom_call" | custom-call | tf_op jit(solution)/shard_map/layers/pallas_call | solution.py:521
  284.9 3.8 reshape.130
  288.6 0.8 copy.53
  289.5 47.8 %all_to_all.15 = bf16[64,3,64,128]{3,2,1,0:T(8,128)(2,1)S(1)} all-to-all(bf16[64,3,64,128]{3,2,1,0:T(8,128)(2,1)S(1)} %bitcast.99), channel_id=1, replica_groups=mesh['section'=2,'tensor'=4,'dp'=16] {'tensor','dp'}, dimensions={0} | all-to-all | bytes 6291456 | tf_op jit(solution)/shard_map/all_to_all | solution.py:617
  337.3 4.8 %all-to-all-start.1 = ((bf16[32,64,896]{2,1,0:T(8,128)(2,1)}), bf16[32,64,896]{2,1,0:T(8,128)(2,1)}, u32[]{:S(2)}, u32[]{:S(2)}) async-start(bf16[32,64,896]{2,1,0:T(8,128)(2,1)} %bitcast.101), calls=%async_computation.1 | async-start | bytes 7340032 | tf_op jit(solution)/shard_map/all_to_all | solution.py:612
  342.1 0.7 convert_reduce_fusion.1
  342.8 1.1 slice_bitcast_fusion
  343.9 1.6 copy_bitcast_fusion
  345.5 45.4 %all-to-all-done.1 = bf16[32,64,896]{2,1,0:T(8,128)(2,1)} async-done(((bf16[32,64,896]{2,1,0:T(8,128)(2,1)}), bf16[32,64,896]{2,1,0:T(8,128)(2,1)}, u32[]{:S(2)}, u32[]{:S(2)}) %all-to-all-start.1) | async-done | bytes 3670048 | tf_op jit(solution)/shard_map/all_to_all | solution.py:612
  390.9 2.6 convert_reduce_fusion
  393.6 0.7 slice_bitcast_fusion.1
  394.3 0.7 copy.56
  394.9 0.6 copy.52
  395.6 0.6 maximum_bitcast_fusion.1
  396.2 1.0 copy.62
  397.2 1.0 copy.63
  (29 shorter events, 1.6 us)
Async XLA Ops:
  7.2 83.0 %all-gather.2.cloned.1.call-start = ((), (), s32[]{:S(2)}) async-start(), calls=%async_computation.3 | async-start | bytes 3784704 | tf_op jit(solution)/shard_map/all_gather | solution.py:597
  15.4 11.6 %copy-start.2 = (s32[1,2,128,8]{2,3,1,0:T(8,128)S(1)}, s32[1,2,128,8]{2,3,1,0:T(8,128)}, u32[]{:S(2)}) copy-start(s32[1,2,128,8]{2,3,1,0:T(8,128)} %param.12) | copy-start | bytes 24580
  15.4 14.3 %copy-start.3 = (s32[2,1,4]{2,1,0:T(1,128)S(1)}, s32[2,1,4]{2,1,0:T(1,128)}, u32[]{:S(2)}) copy-start(s32[2,1,4]{2,1,0:T(1,128)} %param.11) | copy-start | bytes 100
  15.4 53.8 %all-to-all-start = ((bf16[64,3,64,128]{3,2,1,0:T(8,128)(2,1)}), bf16[64,3,64,128]{3,2,1,0:T(8,128)(2,1)S(1)}, u32[]{:S(2)}, u32[]{:S(2)}) async-start(bf16[64,3,64,128]{3,2,1,0:T(8,128)(2,1)} %bitcast.95), calls=%async_computation | async-start | bytes 6291456 | tf_op jit(solution)/shard_map/all_to_all | solution.py:605
  27.1 4.9 %collective-permute-start.1 = (s32[8,128]{1,0:T(8,128)S(1)}, s32[8,128]{1,0:T(8,128)S(1)}, u32[]{:S(2)}, u32[]{:S(2)}) collective-permute-start(s32[8,128]{1,0:T(8,128)S(1)} %select_bitcast_fusion.1), channel_id=1, source_target_pairs={{0,64},{64,0},{1,65},{65,1},{2,66},{66,2},{3,67},{67,3},{4,68},{68... | collective-permute-start | bytes 12296 | tf_op jit(solution)/shard_map/ppermute | solution.py:577
  29.2 3.4 collective-permute-start
  337.3 53.7 %all-to-all-start.1 = ((bf16[32,64,896]{2,1,0:T(8,128)(2,1)}), bf16[32,64,896]{2,1,0:T(8,128)(2,1)}, u32[]{:S(2)}, u32[]{:S(2)}) async-start(bf16[32,64,896]{2,1,0:T(8,128)(2,1)} %bitcast.101), calls=%async_computation.1 | async-start | bytes 7340032 | tf_op jit(solution)/shard_map/all_to_all | solution.py:612
  345.5 50.7 %copy-start.1 = (f32[2,128,1024]{2,1,0:T(8,128)S(1)}, f32[2,128,1024]{2,1,0:T(8,128)}, u32[]{:S(2)}) copy-start(f32[2,128,1024]{2,1,0:T(8,128)} %get-tuple-element.13) | copy-start | bytes 3145732
  345.5 51.7 %copy-start = (f32[2,128,1024]{2,1,0:T(8,128)S(1)}, f32[2,128,1024]{2,1,0:T(8,128)}, u32[]{:S(2)}) copy-start(f32[2,128,1024]{2,1,0:T(8,128)} %get-tuple-element.14) | copy-start | bytes 3145732
Sparse Core Ops, SparseCore 0:
  11.2 78.9 all-gather.1

commit v2 on v1

--- a/solution.py
+++ b/solution.py
@@ -1,3 +1,5 @@
+import math
+
 import jax
 import jax.numpy as jnp
 from jax import lax
@@ -82,12 +84,14 @@
 
 
 def body(
-    dense, experts, first_x, cotangent, routes, cos_ref, sin_ref, seen_ref,
-    out_ref, grad_ref, dense_grad, expert_grad,
+    lengths, piece, own, boundary, routes_own,
+    out_ref, grad_ref, parts, pieces,
+    dense, experts, dense_grad, expert_grad, other, routes, cos_ref, sin_ref, seen_ref,
     xin, uin, turned, first_in, qkv, mixed, middle, chosen, chance, slot_gate,
     rs_send, rs_recv, ag, small, slots, packed, x_rows, og_rows, gate_s, up_s, hid_s,
     y_rows, ret, gg_low, ug_low, gate_grads, resid, gains, router_back, dqkv, swap_out, swap_in,
     rs_ss, rs_rs, ag_ss, ag_rs, sm_ss, sm_rs, d_ss, d_rs, r_ss, r_rs, w_ss, w_rs,
+    a_ss, a_rs, b_ss, b_rs, e_ss, e_rs, g_ss, g_rs, p_ss, p_rs,
 ):
     s = lax.axis_index("section")
     x = lax.axis_index("tensor")
@@ -104,18 +108,43 @@
         return z2 * 4 + y2, ((z // 2) * 2 + z2) * 4 + y2
 
     barrier = pltpu.get_barrier_semaphore()
-    for k in range(1, 4):
-        pl.semaphore_signal(
-            barrier, inc=1, device_id={"tensor": (x + k) % 4}, device_id_type=MESH
-        )
-    for kz, ky in near:
-        peer = spot(kz, ky)[1]
-        if (kz, ky) != (0, 0):
-            pl.semaphore_signal(barrier, inc=1, device_id={"dp": peer}, device_id_type=MESH)
-        pl.semaphore_signal(
-            barrier, inc=1, device_id={"section": 1 - s, "dp": peer}, device_id_type=MESH
-        )
-    pl.semaphore_wait(barrier, 18)
+
+    def greet(k, carry):
+        there, at = (x + k // 16) % 4, (d + k % 16) % 16
+
+        @pl.when(k > 0)
+        def _():
+            pl.semaphore_signal(
+                barrier, inc=1, device_id={"tensor": there, "dp": at}, device_id_type=MESH
+            )
+
+        @pl.when(k < 16)
+        def _():
+            pl.semaphore_signal(
+                barrier, inc=1, device_id={"section": 1 - s, "dp": at}, device_id_type=MESH
+            )
+
+        return carry
+
+    lax.fori_loop(0, 64, greet, 0)
+
+    row = lax.broadcasted_iota(jnp.int32, (ROWS, 128), 0)
+    lane = lax.broadcasted_iota(jnp.int32, (ROWS, 128), 1)
+    start, row_doc, lane_doc, end = 0, 0, 0, 0
+    for k in range(3):
+        size = lengths[s, k]
+        end = end + size
+        start = start + jnp.where(row >= end, size, 0)
+        row_doc = row_doc + jnp.where(row >= end, 1, 0)
+        lane_doc = lane_doc + jnp.where(lane >= end, 1, 0)
+    step = (lane % 32).astype(f32) * (-2.0 / HEAD_SIZE * math.log(rope_base))
+    angles = (row - start).astype(f32) * jnp.exp(step)
+    sine = jnp.sin(angles)
+    cos_ref[...] = jnp.cos(angles)
+    sin_ref[...] = jnp.where(lane % 64 < 32, -sine, sine)
+    seen_ref[...] = jnp.where((row_doc == lane_doc) & (lane <= row), 1.0, 0.0)
+
+    pl.semaphore_wait(barrier, 79)
 
     def remote(src, dst, send, recv, device):
         return pltpu.make_async_remote_copy(
@@ -269,15 +298,162 @@
             swap_out[way] = ag[l, 1 + 2 * way]
             swap_copy(way).start()
 
-    xin[0] = first_x[...]
-    uin[1] = cotangent[...]
+    def block64(index):
+        return pl.ds(pl.multiple_of(index * 64, 64), 64)
+
+    def block128(index):
+        return pl.ds(pl.multiple_of(index * 128, 128), 128)
+
+    left, right = slice(0, 512), slice(512, DENSE)
+
+    def along_y(k):
+        return {"dp": z * 4 + (y + k) % 4}
+
+    def along_z(k):
+        return {"dp": ((z + k) % 4) * 4 + y}
+
+    def spread_copies(part, phase):
+        copies = []
+        for k in range(1, 4):
+            if part == 0:
+                ref = dense.at[s, z, y, :, left] if phase == 0 else dense.at[s, z, :, :, left]
+                device = along_y(k) if phase == 0 else along_z(k)
+            else:
+                ref = dense.at[s, z, y, :, right] if phase == 0 else dense.at[s, :, y, :, right]
+                device = along_z(k) if phase == 0 else along_y(k)
+            n = k - 1
+            copies.append(
+                remote(ref, ref, a_ss.at[part, phase, n], a_rs.at[part, phase, n], device)
+            )
+        return copies
+
+    def sibling_copy(part, k, layer):
+        if part == 0:
+            ref = dense.at[layer, (z + k) % 4, :, :, left]
+        else:
+            ref = dense.at[layer, :, (y + k) % 4, :, right]
+        return remote(ref, ref, b_ss.at[part, k], b_rs.at[part, k], {"section": 1 - s})
+
+    def exchange_copies():
+        return [
+            remote(boundary.at[1 - s], other, b_ss.at[2, 0], b_rs.at[2, 0], {"section": 1 - s}),
+            remote(routes_own.at[1 - s], routes.at[s], b_ss.at[2, 1], b_rs.at[2, 1],
+                   {"section": 1 - s}),
+        ]
+
+    def expert_copy(k, local_only=False):
+        there, at = (x + k // 16) % 4, (d + k % 16) % 16
+        e = there * 8 + (at // 4 % 2) * 4 + at % 4
+        src, dst = own.at[e], experts.at[:, block64(d), block128(x)]
+        if local_only:
+            return pltpu.make_async_copy(src, dst, e_rs.at[0])
+        return remote(src, dst, e_ss.at[k], e_rs.at[k], {"tensor": there, "dp": at})
+
+    def piece_copy(k, local_only=False):
+        there, at = (x + k // 16) % 4, (d + k % 16) % 16
+        src = expert_grad.at[:, block64(at), block128(there)]
+        dst = pieces.at[z // 2, x * 8 + mine]
+        if local_only:
+            return pltpu.make_async_copy(src, dst, p_rs.at[0])
+        return remote(src, dst, p_ss.at[k], p_rs.at[k], {"tensor": there, "dp": at})
+
+    def all_but_own(copy, act):
+        def one(k, carry):
+            getattr(copy(k), act)()
+            return carry
+
+        lax.fori_loop(1, 64, one, 0)
+
+    def push(copy):
+        copy(0, True).start()
+        all_but_own(copy, "start")
+
+    def arrive(copy):
+        copy(0, True).wait()
+        all_but_own(copy, "wait_recv")
+
+    wide = (slice(0, 512), slice(512, 768), slice(768, DENSE))
+
+    def part_copy(l, c, k, rel, local_only=False):
+        at = (d + k) % 16
+        src = dense_grad.at[l, block64(at), wide[c]]
+        dst = parts.at[rel * 16 + d, :, wide[c]]
+        if local_only:
+            return pltpu.make_async_copy(src, dst, g_rs.at[c, 0])
+        return remote(src, dst, g_ss.at[l, c, k], g_rs.at[c, rel * 16 + k],
+                      {"section": l, "dp": at})
+
+    def part_push(l, c):
+        rel = (s + l) % 2
+
+        @pl.when(s == l)
+        def _():
+            part_copy(l, c, 0, 0, True).start()
+
+        @pl.when(s != l)
+        def _():
+            part_copy(l, c, 0, 1).start()
+
+        def one(k, carry):
+            part_copy(l, c, k, rel).start()
+            return carry
+
+        lax.fori_loop(1, 16, one, 0)
+
+    for copy in exchange_copies():
+        copy.start()
+    routes[s] = routes_own[s]
+    dense[s, z, y] = piece[...]
+    for part in range(2):
+        for copy in spread_copies(part, 0):
+            copy.start()
+
+    @pl.when(s == 0)
+    def _():
+        xin[0] = boundary[0]
+
+    @pl.when(s == 1)
+    def _():
+        uin[1] = boundary[1]
+
+    for part in range(2):
+        for copy in spread_copies(part, 0):
+            copy.wait()
+        for copy in spread_copies(part, 1):
+            copy.start()
+        sibling_copy(part, 0, s).start()
+
+    @pl.when(s == 0)
+    def _():
+        push(expert_copy)
+
+    for part in range(2):
+        for k in range(3):
+            spread_copies(part, 1)[k].wait()
+            sibling_copy(part, 3 - k, s).start()
+
+    @pl.when(s == 1)
+    def _():
+        for copy in exchange_copies()[:1]:
+            copy.wait()
+        xin[0] = other[...]
+
+    def weight(l, low, high):
+        return dense[l, :, :, :, low:high].reshape(WIDTH, high - low)
 
     def forward(l, carry):
-        turned[l] = dense[l, :, 768:896].astype(f32).T
+        @pl.when(s != l)
+        def _():
+            for part in range(2):
+                for k in range(4):
+                    sibling_copy(part, k, s).wait()
+            exchange_copies()[1].wait()
+
+        turned[l] = weight(l, 768, 896).astype(f32).T
         values = xin[l]
         first = (values * scale_of(values) * turned[l, 32:33]).astype(bf16)
         first_in[l] = first
-        made = dot(first, dense[l, :, 0:512])
+        made = dot(first, weight(l, 0, 512))
         cos, sin = cos_ref[...], sin_ref[...]
         for c in range(3):
             cut = slice(128 * c, 128 * c + 128)
@@ -293,7 +469,11 @@
                 dot(soft(half(query, b), keys[c], seen).astype(bf16), vals[c]) for b in range(2)
             ]
             mixed[l, :, cut] = jnp.where(low_lanes(), got[0], got[1]).astype(bf16)
-        scatter_start(l, 0, dot_nt(mixed[l], dense[l, :, 512:768]))
+        scatter_start(l, 0, dot_nt(mixed[l], weight(l, 512, 768)))
+
+        @pl.when((s == 1) & (l == 0))
+        def _():
+            push(expert_copy)
 
         experts_iota = lax.broadcasted_iota(jnp.int32, (E, ROWS), 0)
         named = jnp.zeros((E, ROWS), f32)
@@ -330,6 +510,7 @@
 
         @pl.when(s == l)
         def _():
+            arrive(expert_copy)
             for rel in range(2):
                 dispatch_arrived(0, rel)
                 cut = slice(384 * rel, 384 * rel + 384)
@@ -354,6 +535,12 @@
         return carry
 
     lax.fori_loop(0, 2, forward, 0)
+
+    @pl.when(s == 0)
+    def _():
+        for copy in exchange_copies()[:1]:
+            copy.wait()
+        uin[1] = other[...]
 
     def backward(step, carry):
         l = 1 - step
@@ -391,6 +578,7 @@
             expert_grad[0] = dot_tn(x_rows[...], gg_low[...]).astype(bf16)
             expert_grad[1] = dot_tn(x_rows[...], ug_low[...]).astype(bf16)
             expert_grad[2] = dot_tn(og_rows[...], hid_s[...]).astype(bf16)
+            push(piece_copy)
 
         for copy in small_copies(l, 0):
             copy.wait()
@@ -410,7 +598,9 @@
         gather_end(l, 2)
 
         branch = ag[l, 2]
-        mixed_grad = dot(branch, dense[l, :, 512:768]).astype(bf16)
+        dense_grad[l, :, 512:768] = dot_tn(branch, mixed[l]).astype(bf16)
+        part_push(l, 1)
+        mixed_grad = dot(branch, weight(l, 512, 768)).astype(bf16)
         seen = seen_ref[...] > 0
         cos, sin = cos_ref[...], -sin_ref[...]
         left = low_lanes()
@@ -437,9 +627,9 @@
         key_grad = jnp.where(left, key_grads[0], key_grads[1]) * HEAD_SIZE ** (-0.5)
         dqkv[:, 256:384] = turn(key_grad, cos, sin).astype(bf16)
         dqkv[:, 384:512] = jnp.where(left, value_grads[0], value_grads[1]).astype(bf16)
-        scatter_start(l, 3, dot_nt(dqkv[...], dense[l, :, 0:512]))
+        scatter_start(l, 3, dot_nt(dqkv[...], weight(l, 0, 512)))
         dense_grad[l, :, 0:512] = dot_tn(first_in[l], dqkv[...]).astype(bf16)
-        dense_grad[l, :, 512:768] = dot_tn(branch, mixed[l]).astype(bf16)
+        part_push(l, 0)
         back, gain_one = norm_back(xin[l, rows_mine], turned[l, 32:33], scatter_end(l, 3))
         gather_start(l, 3, resid[...] + back)
         gains[l, x, 0:1] = gain_one
@@ -458,6 +648,7 @@
         total = gains[l, 0] + gains[l, 1] + gains[l, 2] + gains[l, 3]
         last = jnp.concatenate([router_grad, total, jnp.zeros((88, WIDTH), f32)], axis=0)
         dense_grad[l, :, 768:896] = last.T.astype(bf16)
+        part_push(l, 2)
         dispatch_copies(l, 1, 1)
         return carry
 
@@ -468,11 +659,33 @@
         ref[1 - s] = swap_in[way].astype(f32)
         for rel in range(2):
             return_copies(s, way, rel, 1)
+    all_but_own(expert_copy, "wait_send")
+    all_but_own(piece_copy, "wait_send")
+    arrive(piece_copy)
+    for c in range(3):
+        part_copy(s, c, 0, 0, True).wait()
+        part_copy(1 - s, c, 0, 1).wait()
+
+        def one(k, carry):
+            part_copy(s, c, k, 0).wait()
+            part_copy(1 - s, c, k, 1).wait()
+            return carry
+
+        lax.fori_loop(1, 16, one, 0)
 
 
 def layers(*operands):
     shape = jax.ShapeDtypeStruct
     scratch = [
+        pltpu.VMEM((2, 4, 4, 64, DENSE), bf16),
+        pltpu.VMEM((3, WIDTH, FF), bf16),
+        pltpu.VMEM((2, WIDTH, DENSE), bf16),
+        pltpu.VMEM((3, WIDTH, FF), bf16),
+        pltpu.VMEM((ROWS, WIDTH), f32),
+        pltpu.VMEM((2, TOPK, ROWS), jnp.int32),
+        pltpu.VMEM((ROWS, 128), f32),
+        pltpu.VMEM((ROWS, 128), f32),
+        pltpu.VMEM((ROWS, 128), f32),
         pltpu.VMEM((3, ROWS, WIDTH), f32),
         pltpu.VMEM((2, ROWS, WIDTH), f32),
         pltpu.VMEM((2, ROWS, WIDTH), f32),
@@ -517,42 +730,44 @@
         pltpu.SemaphoreType.DMA((2, 2, 8)),
         pltpu.SemaphoreType.DMA((2,)),
         pltpu.SemaphoreType.DMA((2,)),
+        pltpu.SemaphoreType.DMA((2, 2, 3)),
+        pltpu.SemaphoreType.DMA((2, 2, 3)),
+        pltpu.SemaphoreType.DMA((3, 4)),
+        pltpu.SemaphoreType.DMA((3, 4)),
+        pltpu.SemaphoreType.DMA((64,)),
+        pltpu.SemaphoreType.DMA((64,)),
+        pltpu.SemaphoreType.DMA((2, 3, 16)),
+        pltpu.SemaphoreType.DMA((3, 32)),
+        pltpu.SemaphoreType.DMA((64,)),
+        pltpu.SemaphoreType.DMA((64,)),
     ]
     return pl.pallas_call(
         body,
         out_shape=(
             shape((2, ROWS, WIDTH), f32),
             shape((2, ROWS, WIDTH), f32),
-            shape((2, WIDTH, DENSE), bf16),
-            shape((3, WIDTH, FF), bf16),
+            shape((32, 64, DENSE), bf16),
+            shape((2, E, 3, 64, 128), bf16),
         ),
-        in_specs=[pl.BlockSpec(memory_space=pltpu.VMEM)] * 8,
-        out_specs=tuple(pl.BlockSpec(memory_space=pltpu.VMEM) for _ in range(4)),
+        in_specs=[
+            pl.BlockSpec(memory_space=pltpu.SMEM),
+            pl.BlockSpec(memory_space=pltpu.VMEM),
+            pl.BlockSpec(memory_space=pl.ANY),
+            pl.BlockSpec(memory_space=pltpu.VMEM),
+            pl.BlockSpec(memory_space=pltpu.VMEM),
+        ],
+        out_specs=(
+            pl.BlockSpec(memory_space=pltpu.VMEM),
+            pl.BlockSpec(memory_space=pltpu.VMEM),
+            pl.BlockSpec(memory_space=pl.ANY),
+            pl.BlockSpec(memory_space=pl.ANY),
+        ),
         scratch_shapes=scratch,
         compiler_params=pltpu.CompilerParams(
             collective_id=0, has_side_effects=True, vmem_limit_bytes=60 * 1024 * 1024
         ),
         name="layers",
     )(*operands)
-
-
-def doc_tables(lengths):
-    doc_ends = jnp.cumsum(lengths)
-    doc_starts = doc_ends - lengths
-    places = jnp.arange(ROWS, dtype=jnp.int32)
-    segment = jnp.sum((places[:, None] >= doc_ends[None, :]).astype(jnp.int32), axis=1)
-    owners = segment[:, None] == jnp.arange(lengths.shape[0], dtype=jnp.int32)[None, :]
-    offset = places - jnp.sum(jnp.where(owners, doc_starts[None, :], 0), axis=1)
-    visible = (segment[:, None] == segment[None, :]) & (places[None, :] <= places[:, None])
-    half_dim = HEAD_SIZE // 2
-    frequency = rope_base ** (-2.0 * jnp.arange(half_dim, dtype=f32) / HEAD_SIZE)
-    angles = offset.astype(f32)[:, None] * frequency[None, :]
-    cos, sin = jnp.cos(angles), jnp.sin(angles)
-    return (
-        jnp.concatenate([cos] * 4, axis=1),
-        jnp.concatenate([-sin, sin, -sin, sin], axis=1),
-        visible.astype(f32),
-    )
 
 
 def local(
@@ -567,20 +782,6 @@
     w_gateup,
     w_down,
 ):
-    s = lax.axis_index("section")
-    low = s == 0
-    swap = [(0, 1), (1, 0)]
-
-    def exchanged(pair):
-        own = jnp.where(low, pair[0], pair[1])
-        sent = jnp.where(low, pair[1], pair[0])
-        got = lax.ppermute(sent, "section", swap)
-        return jnp.where(low, own, got), jnp.where(low, got, own)
-
-    first_x, cotangent = exchanged(boundary[0])
-    routes_here = jnp.stack(exchanged(jnp.swapaxes(routes[0], 1, 2)))
-    cos, sin, seen = doc_tables(jnp.where(low, doc_lengths[0, 0], doc_lengths[1, 0]))
-
     depth = w_query.shape[1]
     piece = jnp.concatenate(
         [
@@ -594,29 +795,14 @@
         ],
         axis=1,
     )
-    dense = lax.all_gather(piece, ("section", "dp"), axis=0, tiled=True)
-    dense = dense.reshape(2, WIDTH, DENSE)
-
     own = jnp.concatenate(
         [jnp.swapaxes(w_gateup[0], 0, 1), jnp.swapaxes(w_down[0], 1, 2)[:, None]], axis=1
     )
-    own = own.reshape(4, 1, 2, 4, 3, 64, 128)
-    own = jnp.broadcast_to(own, (4, 2, 2, 4, 3, 64, 128)).reshape(64, 3, 64, 128)
-    arrived = lax.all_to_all(own, ("tensor", "dp"), split_axis=0, concat_axis=0, tiled=True)
-    experts = arrived.reshape(4, 16, 3, 64, 128).transpose(2, 1, 3, 0, 4).reshape(3, WIDTH, FF)
-
-    outs, grads, dense_grad, expert_grad = layers(
-        dense, experts, first_x, cotangent, routes_here, cos, sin, seen
-    )
-
-    parts = lax.all_to_all(
-        dense_grad.reshape(32, 64, DENSE), ("section", "dp"), split_axis=0, concat_axis=0, tiled=True
+    outs, grads, parts, pieces = layers(
+        doc_lengths[:, 0], piece, own, boundary[0], jnp.swapaxes(routes[0], 1, 2)
     )
     parts = jnp.sum(parts.astype(f32), axis=0)
-    pieces = expert_grad.reshape(3, 16, 64, 4, 128).transpose(3, 1, 0, 2, 4).reshape(64, 3, 64, 128)
-    pieces = lax.all_to_all(pieces, ("tensor", "dp"), split_axis=0, concat_axis=0, tiled=True)
-    pieces = jnp.sum(pieces.reshape(4, 2, 8, 3, 64, 128).astype(f32), axis=1)
-    pieces = pieces.reshape(E, 3, 64, 128)
+    pieces = jnp.sum(pieces.astype(f32), axis=0)
     return (
         outs[None],
         grads[None],

time: 407 us -> 313 us (0.77)
  Pallas kernels: 195 us -> 294 us
  waiting for transfers between devices: 90.1 us -> 0 us
  blocking collectives: 47.8 us -> 0 us
  starting transfers between devices: 17.1 us -> 0 us
  local copies, waits for them, and re-layouts: 28.3 us -> 11.9 us
  between operations: 14.2 us -> 0.71 us
  other arithmetic: 12.8 us -> 6.38 us
    pallas_call x1, Pallas kernels: 195 us -> 294 us  [layers(): pl.pallas_call(body, out_shape=(shape((2, ROWS, WIDTH), f32), shape((2, R...]
    all_to_all x2 -> x0, waiting for transfers between devices: 79.6 us -> none  [the longest x1 45.4 us: local(): lax.all_to_all(dense_grad.reshape(32, 64, DENSE), ('section', 'dp'), spli...]
    all_to_all x1 -> x0, blocking collectives: 47.8 us -> none  [local(): lax.all_to_all(pieces, ('tensor', 'dp'), split_axis=0, concat_axis=0, til...]
    all_to_all x2 -> x0, starting transfers between devices: 16.5 us -> none  [the longest x1 11.6 us: local(): lax.all_to_all(own, ('tensor', 'dp'), split_axis=0, concat_axis=0, tiled=...]
    all_gather x1 -> x0, waiting for transfers between devices: 10.5 us -> none  [local(): dense = lax.all_gather(piece, ('section', 'dp'), axis=0, tiled=True)]
    reshape x3 -> x0, local copies, waits for them, and re-layouts: 10.3 us -> none  [the longest x1 5.73 us: local(): arrived.reshape(4, 16, 3, 64, 128).transpose(2, 1, 3, 0, 4)]
    transpose x2 -> x0, local copies, waits for them, and re-layouts: 5.48 us -> none  [the longest x1 4.71 us: local(): arrived.reshape(4, 16, 3, 64, 128).transpose(2, 1, 3, 0, 4)]
    select_n x4 -> x0, other arithmetic: 4.55 us -> none  [the longest x1 2.48 us: exchanged(): return (jnp.where(low, own, got), jnp.where(low, got, own))]
  transfers between devices with their start and end apart: 5 -> 0, of which waited for: 3 -> 0; matrix products, arithmetic and copies ran while one was open for 6% -> 0% of each run, Pallas kernels for 0% -> 0%
where the time goes in v2:
time: 313 us
  Pallas kernels  294 us (94%)
  local copies, waits for them, and re-layouts  11.9 us (4%)
  other arithmetic  6.38 us (2%)
    pallas_call x1, Pallas kernels, layers(): pl.pallas_call(body, out_shape=(shape((2, ROWS, WIDTH), f32), shape((2, R...  294 us
    unnamed x12, local copies, waits for them, and re-layouts  6.29 us

profile of v2, /device:TPU:0, one launch (start us, length us, event | category | flops | bytes accessed | tf_op | source)
XLA Modules:
  0.0 312.9 jit_solution(4899692232153494419)
XLA Ops:
  0.6 0.8 copy.28
  1.4 0.8 copy.27
  2.2 0.7 slice_bitcast_fusion.8
  2.9 1.5 concatenate.6.piece
  4.4 1.3 copy.34
  5.8 2.3 pad_maximum_fusion.own
  8.1 293.9 %layers.1 = (f32[2,128,1024]{2,1,0:T(8,128)}, f32[2,128,1024]{2,1,0:T(8,128)}, bf16[32,64,896]{2,1,0:T(8,128)(2,1)}, bf16[2,32,3,64,128]{4,3,2,1,0:T(8,128)(2,1)}) custom-call(s32[2,4]{1,0:T(2,128)} %bitcast.65, bf16[64,896]{1,0:T(8,128)(2,1)} %concatenate.6.piece, bf16[32,3,64,128]{3,2,1,0:T(8,128)(2,1)} %pad_maximum_fusion.own, f32[2,128,1024]{2,1,0:T(8,128)} %bitcast.56, ...), custom_call_target="tpu_custom_call" | custom-call | tf_op jit(solution)/shard_map/layers/pallas_call | solution.py:744
  302.0 0.0 copy-start
  302.0 2.7 convert_reduce_fusion
  304.7 0.7 copy.31
  305.4 0.1 slice_bitcast_fusion.7
  305.5 0.6 copy.30
  306.1 0.7 slice_bitcast_fusion.2
  306.8 0.6 maximum_bitcast_fusion
  307.4 0.0 copy-done
  307.4 0.7 convert_reduce_fusion.1
  308.1 1.1 slice_bitcast_fusion.1
  309.2 0.1 slice_bitcast_fusion
  309.3 0.0 copy-start.2
  309.3 0.0 copy-start.1
  309.4 1.5 copy.32
  310.8 0.1 copy-done.2
  310.9 1.0 copy.37
  311.9 0.0 copy-done.1
  311.9 1.0 copy.38
  (3 shorter events, 0.0 us)
Async XLA Ops:
  302.0 5.4 %copy-start = (bf16[2,32,3,64,128]{4,3,2,1,0:T(8,128)(2,1)S(1)}, bf16[2,32,3,64,128]{4,3,2,1,0:T(8,128)(2,1)}, u32[]{:S(2)}) copy-start(bf16[2,32,3,64,128]{4,3,2,1,0:T(8,128)(2,1)} %get-tuple-element.16) | copy-start | bytes 9437188
  309.3 1.6 copy-start.2
  309.3 2.5 copy-start.1

commit v3 on v2

--- a/solution.py
+++ b/solution.py
@@ -38,6 +38,12 @@
     return lax.dot_general(a, b, (((0,), (0,)), ((), ())), preferred_element_type=f32)
 
 
+def unit(rows, columns, shift):
+    row = lax.broadcasted_iota(jnp.int32, (rows, columns), 0)
+    column = lax.broadcasted_iota(jnp.int32, (rows, columns), 1)
+    return (row + shift == column).astype(bf16)
+
+
 def scale_of(values):
     return lax.rsqrt(jnp.mean(values * values, axis=1, keepdims=True) + epsilon)
 
@@ -84,14 +90,15 @@
 
 
 def body(
-    lengths, piece, own, boundary, routes_own,
+    lengths, query_own, keyval_own, out_own, router_own, gains_own, gateup_own, down_own,
+    boundary, routes_own,
     out_ref, grad_ref, parts, pieces,
-    dense, experts, dense_grad, expert_grad, other, routes, cos_ref, sin_ref, seen_ref,
+    own, dense, experts, dense_grad, shared, expert_grad, other, routes, cos_ref, sin_ref, seen_ref,
     xin, uin, turned, first_in, qkv, mixed, middle, chosen, chance, slot_gate,
     rs_send, rs_recv, ag, small, slots, packed, x_rows, og_rows, gate_s, up_s, hid_s,
     y_rows, ret, gg_low, ug_low, gate_grads, resid, gains, router_back, dqkv, swap_out, swap_in,
     rs_ss, rs_rs, ag_ss, ag_rs, sm_ss, sm_rs, d_ss, d_rs, r_ss, r_rs, w_ss, w_rs,
-    a_ss, a_rs, b_ss, b_rs, e_ss, e_rs, g_ss, g_rs, p_ss, p_rs,
+    a_ss, a_rs, b_ss, b_rs, e_ss, e_rs, g_ss, g_rs, p_ss, p_rs, h_ss, h_rs, c_ss,
 ):
     s = lax.axis_index("section")
     x = lax.axis_index("tensor")
@@ -118,15 +125,14 @@
                 barrier, inc=1, device_id={"tensor": there, "dp": at}, device_id_type=MESH
             )
 
-        @pl.when(k < 16)
-        def _():
-            pl.semaphore_signal(
-                barrier, inc=1, device_id={"section": 1 - s, "dp": at}, device_id_type=MESH
-            )
-
         return carry
 
     lax.fori_loop(0, 64, greet, 0)
+    for kz, ky in near:
+        pl.semaphore_signal(
+            barrier, inc=1, device_id={"section": 1 - s, "dp": spot(kz, ky)[1]},
+            device_id_type=MESH,
+        )
 
     row = lax.broadcasted_iota(jnp.int32, (ROWS, 128), 0)
     lane = lax.broadcasted_iota(jnp.int32, (ROWS, 128), 1)
@@ -144,7 +150,7 @@
     sin_ref[...] = jnp.where(lane % 64 < 32, -sine, sine)
     seen_ref[...] = jnp.where((row_doc == lane_doc) & (lane <= row), 1.0, 0.0)
 
-    pl.semaphore_wait(barrier, 79)
+    pl.semaphore_wait(barrier, 71)
 
     def remote(src, dst, send, recv, device):
         return pltpu.make_async_remote_copy(
@@ -237,16 +243,25 @@
 
     def dispatch_arrived(way, rel):
         target = x_rows if way == 0 else og_rows
-        for n in range(8):
-            dst = target.at[block(rel * 8 + n)]
-            src = packed.at[0, way, block(n)]
-            if rel == 0 and n == 0:
-                pltpu.make_async_copy(
-                    packed.at[0, way, block(mine)], target.at[block(mine)], d_rs.at[way, 0]
-                ).wait()
-            else:
-                remote(src, dst, d_ss.at[0, way, n], d_rs.at[way, rel * 8 + n],
-                       {"dp": spot(0, 1)[1]}).wait_recv()
+
+        def far(n):
+            return remote(
+                packed.at[0, way, block(n)], target.at[block(rel * 8 + n)],
+                d_ss.at[0, way, n], d_rs.at[way, rel * 8 + n], {"dp": spot(0, 1)[1]},
+            )
+
+        @pl.when(rel == 0)
+        def _():
+            pltpu.make_async_copy(
+                packed.at[0, way, block(mine)], target.at[block(mine)], d_rs.at[way, 0]
+            ).wait()
+
+        @pl.when(rel != 0)
+        def _():
+            far(0).wait_recv()
+
+        for n in range(1, 8):
+            far(n).wait_recv()
 
     def return_copies(l, way, rel, act):
         for kz, ky in near:
@@ -254,16 +269,24 @@
             n = kz * 4 + ky
             src = y_rows.at[way, block(rel * 8 + i)]
             dst = ret.at[l, way, block(mine)]
-            if rel == 0 and n == 0:
+            def far():
+                return remote(src, dst, r_ss.at[way, rel * 8 + n], r_rs.at[l, way, n],
+                              {"section": (s + rel) % 2, "dp": peer})
+
+            def go():
                 if act == 0:
-                    pltpu.make_async_copy(src, dst, r_rs.at[l, way, 0]).start()
-                continue
-            far = remote(src, dst, r_ss.at[way, rel * 8 + n], r_rs.at[l, way, n],
-                         {"section": (s + rel) % 2, "dp": peer})
-            if act == 0:
-                far.start()
+                    far().start()
+                else:
+                    far().wait_send()
+
+            if n > 0:
+                go()
             else:
-                far.wait_send()
+                pl.when(rel != 0)(go)
+                if act == 0:
+                    @pl.when(rel == 0)
+                    def _():
+                        pltpu.make_async_copy(src, dst, r_rs.at[l, way, 0]).start()
 
     def return_arrived(l, way):
         for kz, ky in near:
@@ -291,7 +314,7 @@
     def keep_result(way, l, ref):
         @pl.when(s == l)
         def _():
-            ref[s] = ag[l, 1 + 2 * way].astype(f32)
+            ref[s] = ag[l, 1 + 2 * way]
 
         @pl.when(s != l)
         def _():
@@ -334,6 +357,10 @@
             ref = dense.at[layer, :, (y + k) % 4, :, right]
         return remote(ref, ref, b_ss.at[part, k], b_rs.at[part, k], {"section": 1 - s})
 
+    def weight_copy(kind):
+        src = gateup_own.at[kind] if kind < 2 else down_own
+        return pltpu.make_async_copy(src, own.at[:, kind], c_ss.at[kind])
+
     def exchange_copies():
         return [
             remote(boundary.at[1 - s], other, b_ss.at[2, 0], b_rs.at[2, 0], {"section": 1 - s}),
@@ -352,21 +379,26 @@
     def piece_copy(k, local_only=False):
         there, at = (x + k // 16) % 4, (d + k % 16) % 16
         src = expert_grad.at[:, block64(at), block128(there)]
-        dst = pieces.at[z // 2, x * 8 + mine]
+        dst = pieces.at[z // 2, :, x * 8 + mine]
         if local_only:
             return pltpu.make_async_copy(src, dst, p_rs.at[0])
         return remote(src, dst, p_ss.at[k], p_rs.at[k], {"tensor": there, "dp": at})
 
-    def all_but_own(copy, act):
-        def one(k, carry):
-            getattr(copy(k), act)()
+    def all_but_own(copy, act, low=1, high=64):
+        def one(n, carry):
+            getattr(copy(n * 13 % 64), act)()
             return carry
 
-        lax.fori_loop(1, 64, one, 0)
-
-    def push(copy):
-        copy(0, True).start()
-        all_but_own(copy, "start")
+        lax.fori_loop(low, high, one, 0)
+
+    def push(copy, low, high):
+        whole = isinstance(low, int) and low == 0
+        if whole:
+            copy(0, True).start()
+        all_but_own(copy, "start", 1 if whole else low, high)
+
+    def push_when(condition, copy, low, high):
+        pl.when(condition)(lambda: push(copy, low, high))
 
     def arrive(copy):
         copy(0, True).wait()
@@ -374,40 +406,53 @@
 
     wide = (slice(0, 512), slice(512, 768), slice(768, DENSE))
 
-    def part_copy(l, c, k, rel, local_only=False):
+    def part_copy(c, k, local_only=False):
         at = (d + k) % 16
-        src = dense_grad.at[l, block64(at), wide[c]]
-        dst = parts.at[rel * 16 + d, :, wide[c]]
+        src = dense_grad.at[s, block64(at), wide[c]]
+        dst = parts.at[d, :, wide[c]]
         if local_only:
             return pltpu.make_async_copy(src, dst, g_rs.at[c, 0])
-        return remote(src, dst, g_ss.at[l, c, k], g_rs.at[c, rel * 16 + k],
-                      {"section": l, "dp": at})
+        return remote(src, dst, g_ss.at[c, k], g_rs.at[c, k], {"dp": at})
+
+    def share_copy(c):
+        return remote(dense_grad.at[1 - s, :, wide[c]], shared.at[:, wide[c]],
+                      h_ss.at[c], h_rs.at[c], {"section": 1 - s})
+
+    def share(l, c):
+        @pl.when(s != l)
+        def _():
+            share_copy(c).start()
 
     def part_push(l, c):
-        rel = (s + l) % 2
-
         @pl.when(s == l)
         def _():
-            part_copy(l, c, 0, 0, True).start()
-
-        @pl.when(s != l)
-        def _():
-            part_copy(l, c, 0, 1).start()
-
-        def one(k, carry):
-            part_copy(l, c, k, rel).start()
-            return carry
-
-        lax.fori_loop(1, 16, one, 0)
+            share_copy(c).wait_recv()
+            both = dense_grad[l, :, wide[c]].astype(f32) + shared[:, wide[c]].astype(f32)
+            dense_grad[l, :, wide[c]] = both.astype(bf16)
+            part_copy(c, 0, True).start()
+
+            def one(k, carry):
+                part_copy(c, k).start()
+                return carry
+
+            lax.fori_loop(1, 16, one, 0)
 
     for copy in exchange_copies():
         copy.start()
+    for kind in range(3):
+        weight_copy(kind).start()
     routes[s] = routes_own[s]
-    dense[s, z, y] = piece[...]
+    dense[s, z, y, :, 0:256] = query_own[...]
+    dense[s, z, y, :, 256:384] = keyval_own[0]
+    dense[s, z, y, :, 384:512] = keyval_own[1]
+    dense[s, z, y, :, 512:768] = out_own[...]
+    last = dot_tn(router_own[...], unit(E, 128, 0)) + dot_tn(gains_own[...], unit(2, 128, E))
+    dense[s, z, y, :, 768:896] = last.astype(bf16)
     for part in range(2):
         for copy in spread_copies(part, 0):
             copy.start()
 
+
     @pl.when(s == 0)
     def _():
         xin[0] = boundary[0]
@@ -419,18 +464,26 @@
     for part in range(2):
         for copy in spread_copies(part, 0):
             copy.wait()
-        for copy in spread_copies(part, 1):
-            copy.start()
-        sibling_copy(part, 0, s).start()
+    for kind in range(3):
+        weight_copy(kind).wait()
+
+    def spread_start():
+        for part in range(2):
+            for copy in spread_copies(part, 1):
+                copy.start()
+            sibling_copy(part, 0, s).start()
+
+    def spread_end():
+        for part in range(2):
+            for k in range(3):
+                spread_copies(part, 1)[k].wait()
+                sibling_copy(part, 3 - k, s).start()
 
     @pl.when(s == 0)
     def _():
-        push(expert_copy)
-
-    for part in range(2):
-        for k in range(3):
-            spread_copies(part, 1)[k].wait()
-            sibling_copy(part, 3 - k, s).start()
+        spread_start()
+        push(expert_copy, 0, 64)
+        spread_end()
 
     @pl.when(s == 1)
     def _():
@@ -446,7 +499,7 @@
         def _():
             for part in range(2):
                 for k in range(4):
-                    sibling_copy(part, k, s).wait()
+                    sibling_copy(part, k, s).wait_recv()
             exchange_copies()[1].wait()
 
         turned[l] = weight(l, 768, 896).astype(f32).T
@@ -471,9 +524,11 @@
             mixed[l, :, cut] = jnp.where(low_lanes(), got[0], got[1]).astype(bf16)
         scatter_start(l, 0, dot_nt(mixed[l], weight(l, 512, 768)))
 
+
         @pl.when((s == 1) & (l == 0))
         def _():
-            push(expert_copy)
+            spread_start()
+            push(expert_copy, 0, 64)
 
         experts_iota = lax.broadcasted_iota(jnp.int32, (E, ROWS), 0)
         named = jnp.zeros((E, ROWS), f32)
@@ -511,9 +566,10 @@
         @pl.when(s == l)
         def _():
             arrive(expert_copy)
-            for rel in range(2):
+            for turn_no in range(2):
+                rel = (l + turn_no) % 2
                 dispatch_arrived(0, rel)
-                cut = slice(384 * rel, 384 * rel + 384)
+                cut = pl.ds(pl.multiple_of(384 * rel, 384), 384)
                 rows = x_rows[cut]
                 gate_part = dot(rows, experts[0])
                 up_part = dot(rows, experts[1])
@@ -523,6 +579,10 @@
                 hid_s[cut] = hidden
                 y_rows[0, cut] = dot_nt(hidden, experts[2]).astype(bf16)
                 return_copies(l, 0, rel, 0)
+
+        @pl.when((s == 1) & (l == 0))
+        def _():
+            spread_end()
 
         return_arrived(l, 0)
         scaled = ret[l, 0].astype(f32) * slot_gate[l]
@@ -559,9 +619,10 @@
 
         @pl.when(s == l)
         def _():
-            for rel in range(2):
+            for turn_no in range(2):
+                rel = (l + turn_no) % 2
                 dispatch_arrived(1, rel)
-                cut = slice(384 * rel, 384 * rel + 384)
+                cut = pl.ds(pl.multiple_of(384 * rel, 384), 384)
                 hidden_grad = dot(og_rows[cut], experts[2])
                 gate_part = gate_s[cut]
                 up_part = up_s[cut]
@@ -578,7 +639,7 @@
             expert_grad[0] = dot_tn(x_rows[...], gg_low[...]).astype(bf16)
             expert_grad[1] = dot_tn(x_rows[...], ug_low[...]).astype(bf16)
             expert_grad[2] = dot_tn(og_rows[...], hid_s[...]).astype(bf16)
-            push(piece_copy)
+            push(piece_copy, 0, 8)
 
         for copy in small_copies(l, 0):
             copy.wait()
@@ -589,17 +650,20 @@
         router_back[...] = dot_tn(logit_low, turned[l, 0:32].astype(bf16))
         return_arrived(l, 1)
         scatter_start(l, 2, dot_tn(chosen[l], ret[l, 1]))
+        push_when(s == l, piece_copy, 8, 16)
         router_grad = dot(logit_low, ag[l, 0])
         arrived = scatter_end(l, 2) + router_back[rows_mine]
         back, gain_two = norm_back(middle[l], turned[l, 33:34], arrived)
         kept = uin[l, rows_mine] + back
         resid[...] = kept
         gather_start(l, 2, kept)
+        push_when(s == l, piece_copy, 16, 24)
         gather_end(l, 2)
 
         branch = ag[l, 2]
         dense_grad[l, :, 512:768] = dot_tn(branch, mixed[l]).astype(bf16)
-        part_push(l, 1)
+        share(l, 1)
+        push_when(s == l, piece_copy, 24, 40)
         mixed_grad = dot(branch, weight(l, 512, 768)).astype(bf16)
         seen = seen_ref[...] > 0
         cos, sin = cos_ref[...], -sin_ref[...]
@@ -628,16 +692,20 @@
         dqkv[:, 256:384] = turn(key_grad, cos, sin).astype(bf16)
         dqkv[:, 384:512] = jnp.where(left, value_grads[0], value_grads[1]).astype(bf16)
         scatter_start(l, 3, dot_nt(dqkv[...], weight(l, 0, 512)))
+        push_when(s == l, piece_copy, 40, 48)
         dense_grad[l, :, 0:512] = dot_tn(first_in[l], dqkv[...]).astype(bf16)
-        part_push(l, 0)
+        share(l, 0)
+        part_push(l, 1)
         back, gain_one = norm_back(xin[l, rows_mine], turned[l, 32:33], scatter_end(l, 3))
         gather_start(l, 3, resid[...] + back)
+        push_when(s == l, piece_copy, 48, 56)
         gains[l, x, 0:1] = gain_one
         gains[l, x, 1:2] = gain_two
         for k in range(1, 4):
             ref = gains.at[l, x]
             remote(ref, ref, sm_ss.at[l, 1, k - 1], sm_rs.at[l, 1, k - 1],
                    {"tensor": (x + k) % 4}).start()
+        part_push(l, 0)
         gather_end(l, 3)
         uin[1 - l] = ag[l, 3].astype(f32)
         keep_result(1, l, grad_ref)
@@ -648,6 +716,8 @@
         total = gains[l, 0] + gains[l, 1] + gains[l, 2] + gains[l, 3]
         last = jnp.concatenate([router_grad, total, jnp.zeros((88, WIDTH), f32)], axis=0)
         dense_grad[l, :, 768:896] = last.T.astype(bf16)
+        push_when(s == l, piece_copy, 56, 64)
+        share(l, 2)
         part_push(l, 2)
         dispatch_copies(l, 1, 1)
         return carry
@@ -656,19 +726,21 @@
 
     for way, ref in ((0, out_ref), (1, grad_ref)):
         swap_copy(way).wait()
-        ref[1 - s] = swap_in[way].astype(f32)
+        ref[1 - s] = swap_in[way]
         for rel in range(2):
-            return_copies(s, way, rel, 1)
+            return_copies(s, way, jnp.int32(rel), 1)
+    for part in range(2):
+        for k in range(4):
+            sibling_copy(part, k, s).wait_send()
     all_but_own(expert_copy, "wait_send")
     all_but_own(piece_copy, "wait_send")
     arrive(piece_copy)
     for c in range(3):
-        part_copy(s, c, 0, 0, True).wait()
-        part_copy(1 - s, c, 0, 1).wait()
+        share_copy(c).wait_send()
+        part_copy(c, 0, True).wait()
 
         def one(k, carry):
-            part_copy(s, c, k, 0).wait()
-            part_copy(1 - s, c, k, 1).wait()
+            part_copy(c, k).wait()
             return carry
 
         lax.fori_loop(1, 16, one, 0)
@@ -677,9 +749,11 @@
 def layers(*operands):
     shape = jax.ShapeDtypeStruct
     scratch = [
+        pltpu.VMEM((E, 3, 64, 128), bf16),
         pltpu.VMEM((2, 4, 4, 64, DENSE), bf16),
         pltpu.VMEM((3, WIDTH, FF), bf16),
         pltpu.VMEM((2, WIDTH, DENSE), bf16),
+        pltpu.VMEM((WIDTH, DENSE), bf16),
         pltpu.VMEM((3, WIDTH, FF), bf16),
         pltpu.VMEM((ROWS, WIDTH), f32),
         pltpu.VMEM((2, TOPK, ROWS), jnp.int32),
@@ -736,25 +810,27 @@
         pltpu.SemaphoreType.DMA((3, 4)),
         pltpu.SemaphoreType.DMA((64,)),
         pltpu.SemaphoreType.DMA((64,)),
-        pltpu.SemaphoreType.DMA((2, 3, 16)),
-        pltpu.SemaphoreType.DMA((3, 32)),
+        pltpu.SemaphoreType.DMA((3, 16)),
+        pltpu.SemaphoreType.DMA((3, 16)),
         pltpu.SemaphoreType.DMA((64,)),
         pltpu.SemaphoreType.DMA((64,)),
+        pltpu.SemaphoreType.DMA((3,)),
+        pltpu.SemaphoreType.DMA((3,)),
+        pltpu.SemaphoreType.DMA((3,)),
     ]
     return pl.pallas_call(
         body,
         out_shape=(
-            shape((2, ROWS, WIDTH), f32),
-            shape((2, ROWS, WIDTH), f32),
-            shape((32, 64, DENSE), bf16),
-            shape((2, E, 3, 64, 128), bf16),
+            shape((2, ROWS, WIDTH), bf16),
+            shape((2, ROWS, WIDTH), bf16),
+            shape((16, 64, DENSE), bf16),
+            shape((2, 3, E, 64, 128), bf16),
         ),
         in_specs=[
             pl.BlockSpec(memory_space=pltpu.SMEM),
-            pl.BlockSpec(memory_space=pltpu.VMEM),
-            pl.BlockSpec(memory_space=pl.ANY),
-            pl.BlockSpec(memory_space=pltpu.VMEM),
-            pl.BlockSpec(memory_space=pltpu.VMEM),
+            *[pl.BlockSpec(memory_space=pltpu.VMEM) for _ in range(5)],
+            *[pl.BlockSpec(memory_space=pl.ANY) for _ in range(2)],
+            *[pl.BlockSpec(memory_space=pltpu.VMEM) for _ in range(2)],
         ],
         out_specs=(
             pl.BlockSpec(memory_space=pltpu.VMEM),
@@ -782,37 +858,22 @@
     w_gateup,
     w_down,
 ):
-    depth = w_query.shape[1]
-    piece = jnp.concatenate(
-        [
-            w_query[0],
-            key_value_weight[0, 0],
-            key_value_weight[0, 1],
-            w_out[0].T,
-            w_router[0],
-            norm_gains[0].T,
-            jnp.zeros((depth, DENSE - 802), bf16),
-        ],
-        axis=1,
-    )
-    own = jnp.concatenate(
-        [jnp.swapaxes(w_gateup[0], 0, 1), jnp.swapaxes(w_down[0], 1, 2)[:, None]], axis=1
-    )
     outs, grads, parts, pieces = layers(
-        doc_lengths[:, 0], piece, own, boundary[0], jnp.swapaxes(routes[0], 1, 2)
+        doc_lengths[:, 0], w_query[0], key_value_weight[0], w_out[0].T, w_router[0].T, norm_gains[0],
+        w_gateup[0], jnp.swapaxes(w_down[0], 1, 2), boundary[0], jnp.swapaxes(routes[0], 1, 2),
     )
     parts = jnp.sum(parts.astype(f32), axis=0)
-    pieces = jnp.sum(pieces.astype(f32), axis=0)
+    pieces = pieces.astype(f32)
     return (
-        outs[None],
-        grads[None],
+        outs.astype(f32)[None],
+        grads.astype(f32)[None],
         parts[:, 800:802].T[None],
         parts[:, 0:256][None],
         jnp.stack([parts[:, 256:384], parts[:, 384:512]])[None],
         parts[:, 512:768].T[None],
         parts[:, 768:800][None],
-        jnp.swapaxes(pieces[:, 0:2], 0, 1)[None],
-        jnp.swapaxes(pieces[:, 2], 1, 2)[None],
+        (pieces[0, 0:2] + pieces[1, 0:2])[None],
+        jnp.swapaxes(pieces[0, 2] + pieces[1, 2], 1, 2)[None],
     )
 
 

time: 313 us -> 289 us (0.923)
  Pallas kernels: 294 us -> 277 us
  local copies, waits for them, and re-layouts: 11.9 us -> 2.07 us
    pallas_call x1, Pallas kernels: 294 us -> 277 us  [layers(): pl.pallas_call(body, out_shape=(shape((2, ROWS, WIDTH), bf16), shape((2,...]
    unnamed x12 -> x3, local copies, waits for them, and re-layouts: 6.29 us -> 0.68 us
    broadcast_in_dim x0 -> x2, other arithmetic: none -> 3.92 us  [the longest x1 2.76 us: local(): grads.astype(f32)[None]]
where the time goes in v3:
time: 289 us
  Pallas kernels  277 us (96%)
  other arithmetic  8.94 us (3%)
    pallas_call x1, Pallas kernels, layers(): pl.pallas_call(body, out_shape=(shape((2, ROWS, WIDTH), bf16), shape((2,...  277 us

profile of v3, /device:TPU:0, one launch (start us, length us, event | category | flops | bytes accessed | tf_op | source)
XLA Modules:
  0.0 288.5 jit_solution(18000016883322160436)
XLA Ops:
  0.6 276.9 %layers.1 = (bf16[2,128,1024]{2,1,0:T(8,128)(2,1)}, bf16[2,128,1024]{2,1,0:T(8,128)(2,1)}, bf16[16,64,896]{2,1,0:T(8,128)(2,1)}, bf16[2,3,32,64,128]{4,3,2,1,0:T(8,128)(2,1)}) custom-call(s32[2,4]{1,0:T(2,128)} %bitcast.55, bf16[64,256]{1,0:T(8,128)(2,1)} %bitcast.50, bf16[2,64,128]{2,1,0:T(8,128)(2,1)} %bitcast.51, bf16[64,256]{1,0:T(8,128)(2,1)} %bitcast.52, ...), custom_call_target="tpu_custom_call" | custom-call | tf_op jit(solution)/shard_map/layers/pallas_call | solution.py:821
  277.5 1.8 convert_reduce_fusion
  279.3 0.0 copy-start
  279.3 0.7 copy.20
  280.0 0.1 slice_bitcast_fusion.5
  280.1 0.6 copy.19
  280.7 0.7 slice_bitcast_fusion
  281.4 0.6 maximum_bitcast_fusion
  282.0 2.8 bitcast_convert_fusion
  284.8 0.0 copy-done
  284.8 0.7 convert_element_type.9
  285.5 1.2 fusion
  286.7 1.9 slice_add_fusion
  (2 shorter events, 0.0 us)
Async XLA Ops:
  279.3 5.5 %copy-start = (bf16[2,3,32,64,128]{4,3,2,1,0:T(8,128)(2,1)S(1)}, bf16[2,3,32,64,128]{4,3,2,1,0:T(8,128)(2,1)}, u32[]{:S(2)}) copy-start(bf16[2,3,32,64,128]{4,3,2,1,0:T(8,128)(2,1)} %get-tuple-element.16) | copy-start | bytes 9437188

commit v4 on v3

--- a/solution.py
+++ b/solution.py
@@ -96,7 +96,7 @@
     own, dense, experts, dense_grad, shared, expert_grad, other, routes, cos_ref, sin_ref, seen_ref,
     xin, uin, turned, first_in, qkv, mixed, middle, chosen, chance, slot_gate,
     rs_send, rs_recv, ag, small, slots, packed, x_rows, og_rows, gate_s, up_s, hid_s,
-    y_rows, ret, gg_low, ug_low, gate_grads, resid, gains, router_back, dqkv, swap_out, swap_in,
+    y_rows, ret, gu_low, probs, gate_grads, resid, gains, router_back, dqkv, swap_out, swap_in,
     rs_ss, rs_rs, ag_ss, ag_rs, sm_ss, sm_rs, d_ss, d_rs, r_ss, r_rs, w_ss, w_rs,
     a_ss, a_rs, b_ss, b_rs, e_ss, e_rs, g_ss, g_rs, p_ss, p_rs, h_ss, h_rs, c_ss,
 ):
@@ -105,14 +105,21 @@
     d = lax.axis_index("dp")
     z, y = d // 4, d % 4
     zz = z % 2
-    mine = zz * 4 + y
+    mine = zz * 4 + (y + 2 * (z // 2)) % 4
     rows_mine = pl.ds(pl.multiple_of(x * PART, PART), PART)
     experts_mine = pl.ds(pl.multiple_of(x * LOCAL, LOCAL), LOCAL)
-    near = [(kz, ky) for kz in range(2) for ky in range(4)]
-
-    def spot(kz, ky):
-        z2, y2 = (zz + kz) % 2, (y + ky) % 4
-        return z2 * 4 + y2, ((z // 2) * 2 + z2) * 4 + y2
+    odd = (y + z) % 2
+    steps = (
+        (0, 0), (1, 0), (3, 0), (0, 1), (0, 3),
+        (1 + 2 * odd, 1 + 2 * odd), (3 - 2 * odd, 1 + 2 * odd), (2 - 2 * odd, 2 * odd),
+    )
+
+    def holder(n):
+        y2, z2 = (y + steps[n][0]) % 4, (z + steps[n][1]) % 4
+        return z2 % 2 * 4 + (y2 + 2 * (z2 // 2)) % 4, z2 * 4 + y2
+
+    def sender(n):
+        return (z + 4 - steps[n][1]) % 4 * 4 + (y + 4 - steps[n][0]) % 4
 
     barrier = pltpu.get_barrier_semaphore()
 
@@ -128,10 +135,9 @@
         return carry
 
     lax.fori_loop(0, 64, greet, 0)
-    for kz, ky in near:
+    for peer in [holder(n)[1] for n in range(8)] + [sender(5), sender(6)]:
         pl.semaphore_signal(
-            barrier, inc=1, device_id={"section": 1 - s, "dp": spot(kz, ky)[1]},
-            device_id_type=MESH,
+            barrier, inc=1, device_id={"section": 1 - s, "dp": peer}, device_id_type=MESH
         )
 
     row = lax.broadcasted_iota(jnp.int32, (ROWS, 128), 0)
@@ -150,7 +156,7 @@
     sin_ref[...] = jnp.where(lane % 64 < 32, -sine, sine)
     seen_ref[...] = jnp.where((row_doc == lane_doc) & (lane <= row), 1.0, 0.0)
 
-    pl.semaphore_wait(barrier, 71)
+    pl.semaphore_wait(barrier, 73)
 
     def remote(src, dst, send, recv, device):
         return pltpu.make_async_remote_copy(
@@ -160,7 +166,7 @@
 
     def scatter_copies(l, j):
         copies = []
-        for k in range(1, 4):
+        for k in (2, 1, 3):
             p = (x + k) % 4
             src = rs_send.at[l, j, pl.ds(pl.multiple_of(p * PART, PART), PART)]
             copies.append(
@@ -184,7 +190,7 @@
 
     def gather_copies(l, j):
         copies = []
-        for k in range(1, 4):
+        for k in (2, 1, 3):
             ref = ag.at[l, j, rows_mine]
             copies.append(
                 remote(ref, ref, ag_ss.at[l, j, k - 1], ag_rs.at[l, j, k - 1],
@@ -217,11 +223,10 @@
     def dispatch_copies(l, way, act):
         rel = (s + l) % 2
         target = x_rows if way == 0 else og_rows
-        for kz, ky in near:
-            i, peer = spot(kz, ky)
-            n = kz * 4 + ky
+        for n in (5, 6, 7, 1, 2, 3, 4, 0):
+            i, peer = holder(n)
             src = packed.at[l, way, block(i)]
-            dst = target.at[block(rel * 8 + mine)]
+            dst = target.at[block(rel * 8 + n)]
             far = remote(src, dst, d_ss.at[l, way, n], d_rs.at[way, rel * 8 + n],
                          {"section": l, "dp": peer})
             if n == 0:
@@ -247,13 +252,13 @@
         def far(n):
             return remote(
                 packed.at[0, way, block(n)], target.at[block(rel * 8 + n)],
-                d_ss.at[0, way, n], d_rs.at[way, rel * 8 + n], {"dp": spot(0, 1)[1]},
+                d_ss.at[0, way, n], d_rs.at[way, rel * 8 + n], {"dp": holder(1)[1]},
             )
 
         @pl.when(rel == 0)
         def _():
             pltpu.make_async_copy(
-                packed.at[0, way, block(mine)], target.at[block(mine)], d_rs.at[way, 0]
+                packed.at[0, way, block(mine)], target.at[block(0)], d_rs.at[way, 0]
             ).wait()
 
         @pl.when(rel != 0)
@@ -264,10 +269,9 @@
             far(n).wait_recv()
 
     def return_copies(l, way, rel, act):
-        for kz, ky in near:
-            i, peer = spot(kz, ky)
-            n = kz * 4 + ky
-            src = y_rows.at[way, block(rel * 8 + i)]
+        for n in (5, 6, 7, 1, 2, 3, 4, 0):
+            peer = sender(n)
+            src = y_rows.at[way, block(rel * 8 + n)]
             dst = ret.at[l, way, block(mine)]
             def far():
                 return remote(src, dst, r_ss.at[way, rel * 8 + n], r_rs.at[l, way, n],
@@ -289,9 +293,8 @@
                         pltpu.make_async_copy(src, dst, r_rs.at[l, way, 0]).start()
 
     def return_arrived(l, way):
-        for kz, ky in near:
-            i, peer = spot(kz, ky)
-            n = kz * 4 + ky
+        for n in range(8):
+            i, peer = holder(n)
             src = y_rows.at[way, block(n)]
             dst = ret.at[l, way, block(i)]
             far = remote(src, dst, r_ss.at[way, n], r_rs.at[l, way, n],
@@ -370,7 +373,7 @@
 
     def expert_copy(k, local_only=False):
         there, at = (x + k // 16) % 4, (d + k % 16) % 16
-        e = there * 8 + (at // 4 % 2) * 4 + at % 4
+        e = there * 8 + at // 4 % 2 * 4 + (at % 4 + 2 * (at // 8)) % 4
         src, dst = own.at[e], experts.at[:, block64(d), block128(x)]
         if local_only:
             return pltpu.make_async_copy(src, dst, e_rs.at[0])
@@ -631,15 +634,14 @@
                     hidden_grad * up_part * sig * (1.0 + gate_part * (1.0 - sig))
                 ).astype(bf16)
                 up_low = (hidden_grad * gate_part * sig).astype(bf16)
-                gg_low[cut] = gate_low
-                ug_low[cut] = up_low
+                gu_low[cut, 0:FF] = gate_low
+                gu_low[cut, FF:2 * FF] = up_low
                 back = dot_nt(gate_low, experts[0]) + dot_nt(up_low, experts[1])
                 y_rows[1, cut] = back.astype(bf16)
                 return_copies(l, 1, rel, 0)
-            expert_grad[0] = dot_tn(x_rows[...], gg_low[...]).astype(bf16)
-            expert_grad[1] = dot_tn(x_rows[...], ug_low[...]).astype(bf16)
-            expert_grad[2] = dot_tn(og_rows[...], hid_s[...]).astype(bf16)
-            push(piece_copy, 0, 8)
+            both = dot_tn(x_rows[...], gu_low[...])
+            expert_grad[0] = both[:, 0:FF].astype(bf16)
+            expert_grad[1] = both[:, FF:2 * FF].astype(bf16)
 
         for copy in small_copies(l, 0):
             copy.wait()
@@ -650,7 +652,12 @@
         router_back[...] = dot_tn(logit_low, turned[l, 0:32].astype(bf16))
         return_arrived(l, 1)
         scatter_start(l, 2, dot_tn(chosen[l], ret[l, 1]))
-        push_when(s == l, piece_copy, 8, 16)
+
+        @pl.when(s == l)
+        def _():
+            expert_grad[2] = dot_tn(og_rows[...], hid_s[...]).astype(bf16)
+            push(piece_copy, 0, 16)
+
         router_grad = dot(logit_low, ag[l, 0])
         arrived = scatter_end(l, 2) + router_back[rows_mine]
         back, gain_two = norm_back(middle[l], turned[l, 33:34], arrived)
@@ -658,17 +665,18 @@
         resid[...] = kept
         gather_start(l, 2, kept)
         push_when(s == l, piece_copy, 16, 24)
+        seen = seen_ref[...] > 0
+        keys = doubled(qkv[l, :, 256:384])
+        for h in range(4):
+            query = qkv[l, :, 128 * (h // 2):128 * (h // 2) + 128]
+            probs[h] = soft(half(query, h % 2), keys[h // 2], seen)
         gather_end(l, 2)
 
         branch = ag[l, 2]
-        dense_grad[l, :, 512:768] = dot_tn(branch, mixed[l]).astype(bf16)
-        share(l, 1)
         push_when(s == l, piece_copy, 24, 40)
         mixed_grad = dot(branch, weight(l, 512, 768)).astype(bf16)
-        seen = seen_ref[...] > 0
         cos, sin = cos_ref[...], -sin_ref[...]
         left = low_lanes()
-        keys = doubled(qkv[l, :, 256:384])
         vals = doubled(qkv[l, :, 384:512])
         key_grads, value_grads = [], []
         for c in range(2):
@@ -677,7 +685,7 @@
             parts, key_grad, value_grad = [], 0.0, 0.0
             for b in range(2):
                 query_half, above_half = half(query, b), half(above, b)
-                prob = soft(query_half, keys[c], seen)
+                prob = probs[2 * c + b]
                 value_grad = value_grad + dot_tn(prob.astype(bf16), above_half)
                 prob_grad = dot_nt(above_half, vals[c])
                 mean = jnp.sum(prob * prob_grad, axis=1, keepdims=True)
@@ -693,6 +701,8 @@
         dqkv[:, 384:512] = jnp.where(left, value_grads[0], value_grads[1]).astype(bf16)
         scatter_start(l, 3, dot_nt(dqkv[...], weight(l, 0, 512)))
         push_when(s == l, piece_copy, 40, 48)
+        dense_grad[l, :, 512:768] = dot_tn(branch, mixed[l]).astype(bf16)
+        share(l, 1)
         dense_grad[l, :, 0:512] = dot_tn(first_in[l], dqkv[...]).astype(bf16)
         share(l, 0)
         part_push(l, 1)
@@ -783,8 +793,8 @@
         pltpu.VMEM((2 * LOCAL * CAP, FF), bf16),
         pltpu.VMEM((2, 2 * LOCAL * CAP, WIDTH), bf16),
         pltpu.VMEM((2, 2, LOCAL * CAP, WIDTH), bf16),
-        pltpu.VMEM((2 * LOCAL * CAP, FF), bf16),
-        pltpu.VMEM((2 * LOCAL * CAP, FF), bf16),
+        pltpu.VMEM((2 * LOCAL * CAP, 2 * FF), bf16),
+        pltpu.VMEM((4, ROWS, ROWS), f32),
         pltpu.VMEM((8, ROWS), f32),
         pltpu.VMEM((PART, WIDTH), f32),
         pltpu.VMEM((2, 4, 8, WIDTH), f32),

time: 289 us -> 270 us (0.934)
  Pallas kernels: 277 us -> 258 us
    pallas_call x1, Pallas kernels: 277 us -> 258 us  [layers(): pl.pallas_call(body, out_shape=(shape((2, ROWS, WIDTH), bf16), shape((2,...]
where the time goes in v4:
time: 270 us
  Pallas kernels  258 us (96%)
  other arithmetic  8.94 us (3%)
    pallas_call x1, Pallas kernels, layers(): pl.pallas_call(body, out_shape=(shape((2, ROWS, WIDTH), bf16), shape((2,...  258 us

profile of v4, /device:TPU:0, one launch (start us, length us, event | category | flops | bytes accessed | tf_op | source)
XLA Modules:
  0.0 270.1 jit_solution(5218943560675519796)
XLA Ops:
  0.6 258.5 %layers.1 = (bf16[2,128,1024]{2,1,0:T(8,128)(2,1)}, bf16[2,128,1024]{2,1,0:T(8,128)(2,1)}, bf16[16,64,896]{2,1,0:T(8,128)(2,1)}, bf16[2,3,32,64,128]{4,3,2,1,0:T(8,128)(2,1)}) custom-call(s32[2,4]{1,0:T(2,128)} %bitcast.55, bf16[64,256]{1,0:T(8,128)(2,1)} %bitcast.50, bf16[2,64,128]{2,1,0:T(8,128)(2,1)} %bitcast.51, bf16[64,256]{1,0:T(8,128)(2,1)} %bitcast.52, ...), custom_call_target="tpu_custom_call" | custom-call | tf_op jit(solution)/shard_map/layers/pallas_call | solution.py:831
  259.1 1.8 convert_reduce_fusion
  260.9 0.0 copy-start
  260.9 0.7 copy.20
  261.6 0.1 slice_bitcast_fusion.5
  261.7 0.6 copy.19
  262.3 0.7 slice_bitcast_fusion
  263.0 0.6 maximum_bitcast_fusion
  263.6 2.8 %bitcast_convert_fusion = (f32[1,2,128,1024]{3,2,1,0:T(8,128)}, f32[1,2,128,1024]{3,2,1,0:T(8,128)}) fusion(bf16[2,128,1024]{2,1,0:T(8,128)(2,1)} %get-tuple-element.14, bf16[2,128,1024]{2,1,0:T(8,128)(2,1)} %get-tuple-element.13), kind=kLoop, calls=%fused_computation.4 | loop fusion | flops 524288 | bytes 3145728 | tf_op jit(solution)/shard_map/broadcast_in_dim | solution.py:879
  266.4 0.0 copy-done
  266.4 0.7 convert_element_type.9
  267.1 1.2 fusion
  268.3 1.9 slice_add_fusion
  (2 shorter events, 0.0 us)
Async XLA Ops:
  260.9 5.5 %copy-start = (bf16[2,3,32,64,128]{4,3,2,1,0:T(8,128)(2,1)S(1)}, bf16[2,3,32,64,128]{4,3,2,1,0:T(8,128)(2,1)}, u32[]{:S(2)}) copy-start(bf16[2,3,32,64,128]{4,3,2,1,0:T(8,128)(2,1)} %get-tuple-element.16) | copy-start | bytes 9437188

commit v5 on v4

--- a/solution.py
+++ b/solution.py
@@ -530,7 +530,6 @@
 
         @pl.when((s == 1) & (l == 0))
         def _():
-            spread_start()
             push(expert_copy, 0, 64)
 
         experts_iota = lax.broadcasted_iota(jnp.int32, (E, ROWS), 0)
@@ -556,6 +555,7 @@
         second = ag[l, 0]
         packed[l, 0] = dot(chosen[l], second).astype(bf16)
         dispatch_copies(l, 0, 0)
+        pl.when((s == 1) & (l == 0))(spread_start)
         logits = dot_nt(turned[l, 0:32].astype(bf16), second)
         logits = jnp.where(named > 0, logits, masked_score)
         raised = jnp.where(named > 0, jnp.exp(logits - jnp.max(logits, axis=0, keepdims=True)), 0.0)

time: 270 us -> 269 us (level)
  no operation moved by 1% of the time
where the time goes in v5:
time: 269 us
  Pallas kernels  258 us (96%)
  other arithmetic  8.94 us (3%)
    pallas_call x1, Pallas kernels, layers(): pl.pallas_call(body, out_shape=(shape((2, ROWS, WIDTH), bf16), shape((2,...  258 us

profile of v5, /device:TPU:0, one launch (start us, length us, event | category | flops | bytes accessed | tf_op | source)
XLA Modules:
  0.0 269.2 jit_solution(16307585337920912547)
XLA Ops:
  0.6 257.5 %layers.1 = (bf16[2,128,1024]{2,1,0:T(8,128)(2,1)}, bf16[2,128,1024]{2,1,0:T(8,128)(2,1)}, bf16[16,64,896]{2,1,0:T(8,128)(2,1)}, bf16[2,3,32,64,128]{4,3,2,1,0:T(8,128)(2,1)}) custom-call(s32[2,4]{1,0:T(2,128)} %bitcast.55, bf16[64,256]{1,0:T(8,128)(2,1)} %bitcast.50, bf16[2,64,128]{2,1,0:T(8,128)(2,1)} %bitcast.51, bf16[64,256]{1,0:T(8,128)(2,1)} %bitcast.52, ...), custom_call_target="tpu_custom_call" | custom-call | tf_op jit(solution)/shard_map/layers/pallas_call | solution.py:831
  258.2 1.8 convert_reduce_fusion
  259.9 0.0 copy-start
  260.0 0.7 copy.20
  260.6 0.1 slice_bitcast_fusion.5
  260.7 0.6 copy.19
  261.4 0.7 slice_bitcast_fusion
  262.0 0.6 maximum_bitcast_fusion
  262.7 2.8 %bitcast_convert_fusion = (f32[1,2,128,1024]{3,2,1,0:T(8,128)}, f32[1,2,128,1024]{3,2,1,0:T(8,128)}) fusion(bf16[2,128,1024]{2,1,0:T(8,128)(2,1)} %get-tuple-element.14, bf16[2,128,1024]{2,1,0:T(8,128)(2,1)} %get-tuple-element.13), kind=kLoop, calls=%fused_computation.4 | loop fusion | flops 524288 | bytes 3145728 | tf_op jit(solution)/shard_map/broadcast_in_dim | solution.py:879
  265.4 0.0 copy-done
  265.4 0.7 convert_element_type.9
  266.2 1.2 fusion
  267.3 1.9 slice_add_fusion
  (2 shorter events, 0.0 us)
Async XLA Ops:
  259.9 5.5 %copy-start = (bf16[2,3,32,64,128]{4,3,2,1,0:T(8,128)(2,1)S(1)}, bf16[2,3,32,64,128]{4,3,2,1,0:T(8,128)(2,1)}, u32[]{:S(2)}) copy-start(bf16[2,3,32,64,128]{4,3,2,1,0:T(8,128)(2,1)} %get-tuple-element.16) | copy-start | bytes 9437188

commit v6 on v5

--- a/solution.py
+++ b/solution.py
@@ -96,7 +96,7 @@
     own, dense, experts, dense_grad, shared, expert_grad, other, routes, cos_ref, sin_ref, seen_ref,
     xin, uin, turned, first_in, qkv, mixed, middle, chosen, chance, slot_gate,
     rs_send, rs_recv, ag, small, slots, packed, x_rows, og_rows, gate_s, up_s, hid_s,
-    y_rows, ret, gu_low, probs, gate_grads, resid, gains, router_back, dqkv, swap_out, swap_in,
+    y_rows, ret, gu_low, probs, led, gate_grads, resid, gains, router_back, dqkv, swap_out, swap_in,
     rs_ss, rs_rs, ag_ss, ag_rs, sm_ss, sm_rs, d_ss, d_rs, r_ss, r_rs, w_ss, w_rs,
     a_ss, a_rs, b_ss, b_rs, e_ss, e_rs, g_ss, g_rs, p_ss, p_rs, h_ss, h_rs, c_ss,
 ):
@@ -565,6 +565,7 @@
             cut = slice(CAP * i, CAP * i + CAP)
             weighted = chosen[l, cut].astype(f32) * gate[i:i + 1]
             slot_gate[l, cut] = jnp.sum(weighted, axis=1, keepdims=True)
+            led[cut] = weighted.astype(bf16)
 
         @pl.when(s == l)
         def _():
@@ -588,8 +589,7 @@
             spread_end()
 
         return_arrived(l, 0)
-        scaled = ret[l, 0].astype(f32) * slot_gate[l]
-        scatter_start(l, 1, dot_tn(chosen[l], scaled.astype(bf16)))
+        scatter_start(l, 1, dot_tn(led[...], ret[l, 0]))
         gather_start(l, 1, middle[l] + scatter_end(l, 1))
         gather_end(l, 1)
         xin[l + 1] = ag[l, 1].astype(f32)
@@ -795,6 +795,7 @@
         pltpu.VMEM((2, 2, LOCAL * CAP, WIDTH), bf16),
         pltpu.VMEM((2 * LOCAL * CAP, 2 * FF), bf16),
         pltpu.VMEM((4, ROWS, ROWS), f32),
+        pltpu.VMEM((LOCAL * CAP, ROWS), bf16),
         pltpu.VMEM((8, ROWS), f32),
         pltpu.VMEM((PART, WIDTH), f32),
         pltpu.VMEM((2, 4, 8, WIDTH), f32),

time: 269 us -> 268 us (level)
  no operation moved by 1% of the time
where the time goes in v6:
time: 268 us
  Pallas kernels  256 us (96%)
  other arithmetic  8.94 us (3%)
    pallas_call x1, Pallas kernels, layers(): pl.pallas_call(body, out_shape=(shape((2, ROWS, WIDTH), bf16), shape((2,...  256 us

profile of v6, /device:TPU:0, one launch (start us, length us, event | category | flops | bytes accessed | tf_op | source)
XLA Modules:
  0.0 268.1 jit_solution(8830131243507328949)
XLA Ops:
  0.6 256.4 %layers.1 = (bf16[2,128,1024]{2,1,0:T(8,128)(2,1)}, bf16[2,128,1024]{2,1,0:T(8,128)(2,1)}, bf16[16,64,896]{2,1,0:T(8,128)(2,1)}, bf16[2,3,32,64,128]{4,3,2,1,0:T(8,128)(2,1)}) custom-call(s32[2,4]{1,0:T(2,128)} %bitcast.55, bf16[64,256]{1,0:T(8,128)(2,1)} %bitcast.50, bf16[2,64,128]{2,1,0:T(8,128)(2,1)} %bitcast.51, bf16[64,256]{1,0:T(8,128)(2,1)} %bitcast.52, ...), custom_call_target="tpu_custom_call" | custom-call | tf_op jit(solution)/shard_map/layers/pallas_call | solution.py:832
  257.1 1.8 convert_reduce_fusion
  258.9 0.0 copy-start
  258.9 0.7 copy.20
  259.6 0.1 slice_bitcast_fusion.5
  259.6 0.6 copy.19
  260.3 0.7 slice_bitcast_fusion
  260.9 0.6 maximum_bitcast_fusion
  261.6 2.8 %bitcast_convert_fusion = (f32[1,2,128,1024]{3,2,1,0:T(8,128)}, f32[1,2,128,1024]{3,2,1,0:T(8,128)}) fusion(bf16[2,128,1024]{2,1,0:T(8,128)(2,1)} %get-tuple-element.14, bf16[2,128,1024]{2,1,0:T(8,128)(2,1)} %get-tuple-element.13), kind=kLoop, calls=%fused_computation.4 | loop fusion | flops 524288 | bytes 3145728 | tf_op jit(solution)/shard_map/broadcast_in_dim | solution.py:880
  264.3 0.0 copy-done
  264.3 0.7 convert_element_type.9
  265.1 1.2 fusion
  266.2 1.9 slice_add_fusion
  (2 shorter events, 0.0 us)
Async XLA Ops:
  258.9 5.5 %copy-start = (bf16[2,3,32,64,128]{4,3,2,1,0:T(8,128)(2,1)S(1)}, bf16[2,3,32,64,128]{4,3,2,1,0:T(8,128)(2,1)}, u32[]{:S(2)}) copy-start(bf16[2,3,32,64,128]{4,3,2,1,0:T(8,128)(2,1)} %get-tuple-element.16) | copy-start | bytes 9437188
